TPU v7x, 128 devices: a whole 4x4x4 slice. The times are simulated.
128 devices in a mesh: gx: 8 (over x, core), gy: 16 (over y, z).
Axes of the slice: x: 4, y: 4, z: 4, core: 2. Of those that a mesh axis runs over, the one named last changes fastest.
Arguments:
- fields: float32 [512, 2048, 256], P('gx', 'gy'), may hold values from -4 to 4
- increments: bfloat16 [512, 2048, 256], P('gx', 'gy'), may hold values from -5 to 5
- flow_field: float32 [6, 512, 2048], P(None, 'gx', 'gy'), may hold values from -4 to 4
- brick_owner: int32 [16, 64], P('gx', 'gy'), may hold values from -1 to 895, as said below
Outputs:
- relaid: float32 [896, 32, 32, 256], P(('gx', 'gy'))
Inputs may be any that keep to these rules, and one draw needn't show every extreme that they name: `brick_owner`: -1 marks a solid brick. Every slot 0 to 895 is named by exactly one brick; a slot s lies on device s // 7 counted gx-major. Each brick's owner device has the same gx index as the device that holds the brick in the slab. No two bricks of one device of the slab share an owner device. In every index of gx some device of the slab holds 8 fluid bricks.
All inputs are finite; a program needn't handle non-finite values.
Results may differ from a plain program's by a relative error of at most 0.0003.
Values may be sent and summed in bfloat16 or wider, within the bound.
A program may use at most 192 MiB of HBM per device.

v0:
```python
import math

import jax
import jax.numpy as jnp
from jax import lax
from jax.sharding import PartitionSpec as P

TIME_STEP = 0.1
NOISE_SCALE = math.sqrt(0.1)
FENE_LIMIT = 25.0
SPRING_FLOOR = 0.1


def with_halo(shard, sides, width):
    for axis, dim in sides:
        size, length = (lax.axis_size(axis), shard.shape[dim])
        up = [(i, (i + 1) % size) for i in range(size)]
        down = [(j, i) for i, j in up]
        last = lax.slice_in_dim(shard, length - width, length, axis=dim)
        initial = lax.slice_in_dim(shard, 0, width, axis=dim)
        before = lax.ppermute(last, axis, up)
        after = lax.ppermute(initial, axis, down)
        shard = jnp.concatenate([before, shard, after], axis=dim)
    return shard


def stencil(x_extended, y_extended, flow_parts, kicks):
    centre = x_extended[..., 2:-2, :, :]
    back_x = 1.5 * centre - 2.0 * x_extended[..., 1:-3, :, :] + 0.5 * x_extended[..., :-4, :, :]
    ahead_x = -1.5 * centre + 2.0 * x_extended[..., 3:-1, :, :] - 0.5 * x_extended[..., 4:, :, :]
    back_y = 1.5 * centre - 2.0 * y_extended[..., :, 1:-3, :] + 0.5 * y_extended[..., :, :-4, :]
    ahead_y = -1.5 * centre + 2.0 * y_extended[..., :, 3:-1, :] - 0.5 * y_extended[..., :, 4:, :]
    speed_x = flow_parts[0][..., None]
    speed_y = flow_parts[1][..., None]
    transport = (
        jnp.maximum(speed_x, 0.0) * back_x
        + jnp.minimum(speed_x, 0.0) * ahead_x
        + jnp.maximum(speed_y, 0.0) * back_y
        + jnp.minimum(speed_y, 0.0) * ahead_y
    )
    half_lanes = centre.shape[-1] // 2
    first_part = centre[..., :half_lanes]
    second = centre[..., half_lanes:]
    spring = 1.0 / jnp.maximum(
        1.0 - (first_part * first_part + second * second) / FENE_LIMIT, SPRING_FLOOR
    )
    drift_a = (
        flow_parts[2][..., None] * first_part
        + flow_parts[3][..., None] * second
        - 0.5 * spring * first_part
    )
    drift_b = (
        flow_parts[4][..., None] * first_part
        + flow_parts[5][..., None] * second
        - 0.5 * spring * second
    )
    drift = jnp.concatenate([drift_a, drift_b], axis=-1)
    return (
        centre - TIME_STEP * transport + TIME_STEP * drift + NOISE_SCALE * kicks.astype(jnp.float32)
    )


def split_bricks(block, local_rows, local_cols):
    edge_cells = block.shape[0] // local_rows
    shaped = block.reshape(local_rows, edge_cells, local_cols, edge_cells, block.shape[-1])
    return shaped.transpose(0, 2, 1, 3, 4).reshape(
        local_rows * local_cols, edge_cells, edge_cells, block.shape[-1]
    )


def on_device(fields, increments, flow_field, brick_owner):
    local_rows, local_cols = brick_owner.shape
    edge_cells = fields.shape[0] // local_rows
    brick_count = local_rows * local_cols
    slot_count = 7 * brick_count // 8
    peer_count = lax.axis_size("gy")
    active = brick_owner >= 0
    cell_live = jnp.repeat(jnp.repeat(active.astype(jnp.float32), edge_cells, 0), edge_cells, 1)
    masked = fields * cell_live[:, :, None]
    extended = with_halo(masked, (("gx", 0), ("gy", 1)), 2)
    owner_table = lax.all_gather(brick_owner, "gy", axis=1, tiled=True)
    device = lax.axis_index("gx") * peer_count + lax.axis_index("gy")
    owner_flat = brick_owner.reshape(brick_count)
    target = jnp.where(owner_flat >= 0, owner_flat // slot_count % peer_count, -1)
    match_grid = target[None, :] == jnp.arange(peer_count, dtype=jnp.int32)[:, None]
    chosen = jnp.sum(
        jnp.where(match_grid, jnp.arange(brick_count, dtype=jnp.int32)[None, :], 0), axis=1
    )
    present = jnp.any(match_grid, axis=1)
    wanted = device * slot_count + jnp.arange(slot_count, dtype=jnp.int32)
    column = jnp.arange(owner_table.shape[1], dtype=jnp.int32)
    found_grid = owner_table[None, :, :] == wanted[:, None, None]
    source = jnp.sum(jnp.where(found_grid, (column // local_cols)[None, None, :], 0), axis=(1, 2))
    flow_parts = [flow_field[channel] for channel in range(6)]
    updated = stencil(extended[:, 2:-2], extended[2:-2, :], flow_parts, increments)
    bricks = split_bricks(updated, local_rows, local_cols)
    picked = jnp.take(bricks, chosen, axis=0)
    keep = present.reshape((peer_count,) + (1,) * (bricks.ndim - 1))
    arrived = lax.all_to_all(
        jnp.where(keep, picked, jnp.zeros_like(picked)),
        "gy",
        split_axis=0,
        concat_axis=0,
        tiled=True,
    )
    return jnp.take(arrived, source, axis=0)


def solution(mesh):
    in_specs = (P("gx", "gy", None), P("gx", "gy", None), P(None, "gx", "gy"), P("gx", "gy"))
    out_specs = P(("gx", "gy"), None, None, None)
    return jax.shard_map(
        on_device, mesh=mesh, in_specs=in_specs, out_specs=out_specs, check_vma=False
    )
```

profile of v0, /device:TPU:4, one launch (start us, length us, event | category | flops | bytes accessed | tf_op | source)
XLA Modules:
  0.0 430.1 jit_solution(11835707721184402693)
XLA Ops:
  0.0 0.7 fusion.31
  0.7 0.1 copy.18
  0.9 0.1 reshape.153
  1.1 4.1 broadcast_multiply_fusion
  5.2 3.2 copy-done
  8.5 1.7 collective-permute-start.1
  10.5 0.1 select_reduce_fusion
  10.6 11.1 %multiply_subtract_fusion.1 = (f32[64,128,128]{2,1,0:T(8,128)}, f32[64,128,128]{2,1,0:T(8,128)}) fusion(f32[64,128,256]{2,1,0:T(8,128)} %copy-done, f32[64,128]{1,0:T(8,128)S(1)} %get-tuple-element.18, f32[64,128]{1,0:T(8,128)S(1)} %get-tuple-element.19, f32[64,128]{1,0:T(8,128)S(1)} %get-tuple-element.21, f32[64,128]{1,0:T(8,128)S(1)} %get-tuple-element.22), kind=kLoop, calls=%fused_computation.42 | loop fusion | flops 18874368 | bytes 16908288 | tf_op jit(solution)/shard_map/sub | solution.py:48
  21.8 0.1 pad_maximum_fusion.5
  21.9 2.0 collective-permute-start.2
  23.9 4.7 %collective-permute-start.3 = (f32[68,2,256]{2,1,0:T(2,128)S(1)}, f32[68,2,256]{2,1,0:T(2,128)S(1)}, u32[]{:S(2)}, u32[]{:S(2)}) collective-permute-start(f32[68,2,256]{2,1,0:T(2,128)S(1)} %get-tuple-element.10), channel_id=1, source_target_pairs={{1,0},{2,1},{3,2},{4,3},{5,4},{6,5},{7,6},{8,7},{9,8},{10,9},{11,1... | collective-permute-start | bytes 417800 | tf_op jit(solution)/shard_map/ppermute | solution.py:22
  28.6 0.1 fusion.26
  28.7 3.2 collective-permute-done.2
  31.9 8.1 %maximum_maximum_fusion = (f32[68,130,256]{2,1,0:T(8,128)}, f32[68,130,256]{2,1,0:T(8,128)}) fusion(f32[2,128,256]{2,1,0:T(8,128)S(1)} %collective-permute-done.1, f32[64,128,256]{2,1,0:T(8,128)S(1)} %copy-done.1, f32[2,128,256]{2,1,0:T(8,128)S(1)} %collective-permute-done, f32[68,2,256]{2,1,0:T(2,128)S(1)} %collective-permute-done.2, ...), kind=kLoop, calls=%fused_computation.3 | loop fusion | flops 13578240 | bytes 27295744 | tf_op jit(solution)/shard_map/concatenate | solution.py:23
  40.0 19.1 %fusion.11 = f32[64,128,256]{2,1,0:T(8,128)S(1)} fusion(f32[64,128,256]{2,1,0:T(8,128)S(1)} %copy-done.1, f32[2,128,256]{2,1,0:T(8,128)S(1)} %collective-permute-done.1, f32[2,128,256]{2,1,0:T(8,128)S(1)} %collective-permute-done, f32[68,130,256]{2,1,0:T(8,128)} %get-tuple-element.8, f32[68,130,256]{2,1,0:T(8,128)} %get-tuple-element.7, ...), kind=kLoop, calls=%fused_computation.20 | loop fusion | flops 77594624 | bytes 63569920 | tf_op jit(solution)/shard_map/add | solution.py:59
  59.1 4.1 copy.20
  63.3 11.2 %gather_fusion = f32[16,32,32,256]{3,2,1,0:T(8,128)} fusion(f32[8,32,32,256]{3,2,1,0:T(8,128)} %bitcast.37, s32[1024]{0:T(1024)S(1)} %pad_clamp_fusion.1), kind=kCustom, calls=%fused_computation | custom fusion | bytes 33554496 | tf_op jit(solution)/shard_map/jit(_take)/gather | solution.py:97
  74.5 12.5 %select_select_fusion = f32[16,32,32,256]{3,2,1,0:T(8,128)} fusion(f32[16,32,32,256]{3,2,1,0:T(8,128)} %gather_fusion, pred[16]{0:T(512)(128)(4,1)S(1)} %compare_and_fusion, pred[16]{0:T(512)(128)(4,1)S(1)} %fusion.26), kind=kLoop, calls=%fused_computation.2 | loop fusion | flops 8388608 | bytes 33554464 | tf_op jit(solution)/shard_map/jit(_where)/select_n | solution.py:100
  87.0 6.6 %all-to-all-start = ((f32[16,32,32,256]{3,2,1,0:T(8,128)}), f32[16,32,32,256]{3,2,1,0:T(8,128)}, u32[]{:S(2)}, u32[]{:S(2)}) async-start(f32[16,32,32,256]{3,2,1,0:T(8,128)} %select_select_fusion), calls=%async_computation | async-start | bytes 33554432 | tf_op jit(solution)/shard_map/all_to_all | solution.py:99
  93.7 318.3 %all-gather = s32[16,4,2]{1,2,0:T(2,128)S(1)} all-gather(s32[1,4,2]{1,2,0:T(2,128)S(1)} %bitcast.40), channel_id=1, replica_groups=mesh['gx'=8,'gy'=16] {'gy'}, dimensions={0}, use_global_device_ids=true | all-gather | bytes 544 | tf_op jit(solution)/shard_map/all_gather | solution.py:81
  412.0 0.1 reshape.173
  412.1 0.3 fusion.25
  412.5 9.8 %gather_fusion.1 = f32[7,32,32,256]{3,2,1,0:T(8,128)} fusion(f32[16,32,32,256]{3,2,1,0:T(8,128)} %all-to-all-done, s32[1024]{0:T(1024)S(1)} %pad_clamp_fusion), kind=kCustom, calls=%fused_computation.1 | custom fusion | bytes 14680092 | tf_op jit(solution)/shard_map/jit(_take)/gather | solution.py:106
  422.3 7.8 %broadcast_select_fusion = f32[7,32,32,256]{3,2,1,0:T(8,128)} fusion(f32[7,32,32,256]{3,2,1,0:T(8,128)} %gather_fusion.1, pred[7]{0:T(512)(128)(4,1)S(1)} %compare_and_fusion.2), kind=kLoop, calls=%fused_computation.45 | loop fusion | flops 1835008 | bytes 14680071 | tf_op jit(solution)/shard_map/jit(_take)/select_n | solution.py:106
  (31 shorter events, 0.6 us)
Async XLA Ops:
  1.0 9.2 %copy-start.3 = (s32[2,4]{1,0:T(2,128)S(1)}, s32[2,4]{1,0:T(2,128)}, u32[]{:S(2)}) copy-start(s32[2,4]{1,0:T(2,128)} %param.7) | copy-start | bytes 100
  1.0 9.2 %copy-start.2 = (f32[6,64,128]{2,1,0:T(8,128)S(1)}, f32[6,64,128]{2,1,0:T(8,128)}, u32[]{:S(2)}) copy-start(f32[6,64,128]{2,1,0:T(8,128)} %param.6) | copy-start | bytes 589828
  5.2 3.2 copy-start
  8.5 13.3 %collective-permute-start = (f32[2,128,256]{2,1,0:T(8,128)S(1)}, f32[2,128,256]{2,1,0:T(8,128)S(1)}, u32[]{:S(2)}, u32[]{:S(2)}) collective-permute-start(f32[2,128,256]{2,1,0:T(8,128)S(1)} %get-tuple-element.13), channel_id=1, source_target_pairs={{0,16},{16,32},{32,48},{48,64},{64,80},{80,96},{96,112},{112,0},{1... | collective-permute-start | bytes 786440 | tf_op jit(solution)/shard_map/ppermute | solution.py:21
  8.5 13.3 %collective-permute-start.1 = (f32[2,128,256]{2,1,0:T(8,128)S(1)}, f32[2,128,256]{2,1,0:T(8,128)S(1)}, u32[]{:S(2)}, u32[]{:S(2)}) collective-permute-start(f32[2,128,256]{2,1,0:T(8,128)S(1)} %get-tuple-element.14), channel_id=1, source_target_pairs={{16,0},{32,16},{48,32},{64,48},{80,64},{96,80},{112,96},{0,112},{1... | collective-permute-start | bytes 786440 | tf_op jit(solution)/shard_map/ppermute | solution.py:22
  10.6 11.2 %copy-start.1 = (f32[64,128,256]{2,1,0:T(8,128)S(1)}, f32[64,128,256]{2,1,0:T(8,128)}, u32[]{:S(2)}) copy-start(f32[64,128,256]{2,1,0:T(8,128)} %copy-done) | copy-start | bytes 25165828
  21.9 10.0 %collective-permute-start.2 = (f32[68,2,256]{2,1,0:T(2,128)S(1)}, f32[68,2,256]{2,1,0:T(2,128)S(1)}, u32[]{:S(2)}, u32[]{:S(2)}) collective-permute-start(f32[68,2,256]{2,1,0:T(2,128)S(1)} %get-tuple-element.9), channel_id=1, source_target_pairs={{0,1},{1,2},{2,3},{3,4},{4,5},{5,6},{6,7},{7,8},{8,9},{9,10},{10,1... | collective-permute-start | bytes 417800 | tf_op jit(solution)/shard_map/ppermute | solution.py:21
  23.9 8.0 %collective-permute-start.3 = (f32[68,2,256]{2,1,0:T(2,128)S(1)}, f32[68,2,256]{2,1,0:T(2,128)S(1)}, u32[]{:S(2)}, u32[]{:S(2)}) collective-permute-start(f32[68,2,256]{2,1,0:T(2,128)S(1)} %get-tuple-element.10), channel_id=1, source_target_pairs={{1,0},{2,1},{3,2},{4,3},{5,4},{6,5},{7,6},{8,7},{9,8},{10,9},{11,1... | collective-permute-start | bytes 417800 | tf_op jit(solution)/shard_map/ppermute | solution.py:22
  87.0 325.4 %all-to-all-start = ((f32[16,32,32,256]{3,2,1,0:T(8,128)}), f32[16,32,32,256]{3,2,1,0:T(8,128)}, u32[]{:S(2)}, u32[]{:S(2)}) async-start(f32[16,32,32,256]{3,2,1,0:T(8,128)} %select_select_fusion), calls=%async_computation | async-start | bytes 33554432 | tf_op jit(solution)/shard_map/all_to_all | solution.py:99
where the time goes:
time: 431 us; the launch traced here: 430 us
  blocking collectives  318 us (74%)
  other arithmetic  64.2 us (15%)
  local copies, waits for them, and re-layouts  29.2 us (7%)
  starting transfers between devices  15 us (3%)
    all_gather x1, blocking collectives, on_device(): owner_table = lax.all_gather(brick_owner, 'gy', axis=1, tiled=True)  318 us
    add x1, other arithmetic, stencil(): centre - TIME_STEP * transport + TIME_STEP * drift  19.1 us
    select_n x1, other arithmetic, on_device(): jnp.where(keep, picked, jnp.zeros_like(picked))  12.5 us
    gather x1, local copies, waits for them, and re-layouts, on_device(): picked = jnp.take(bricks, chosen, axis=0)  11.2 us
    sub x1, other arithmetic, stencil(): flow_parts[2][..., None] * first_part + flow_parts[3][..., None] * second  11.1 us
    gather x1, local copies, waits for them, and re-layouts, on_device(): return jnp.take(arrived, source, axis=0)  9.84 us
  transfers between devices with their start and end apart: 5, of which 1 were waited for; matrix products, arithmetic and copies ran while one was open for 3% of the time, Pallas kernels for 0%

commit v1 on v0

v1 whole, which is shorter than its diff:
```python
import functools
import math

import jax
import jax.numpy as jnp
from jax import lax
from jax.experimental import pallas as pl
from jax.experimental.pallas import tpu as pltpu
from jax.sharding import PartitionSpec as P

MESH = pl.DeviceIdType.MESH
NOISE_SCALE = math.sqrt(0.1)
CODE_MAX = 32767.0
VALUE_MAX = 24.0
EDGE = 32
PITCH = 144
NX, NY = 64, 128


def encode(value):
    root = jnp.maximum(jnp.abs(value), 1e-30) * (1.0 / VALUE_MAX)
    for _ in range(3):
        root = root * lax.rsqrt(root)
    code = jnp.minimum(root * CODE_MAX + 0.5, CODE_MAX)
    return jnp.where(value < 0.0, -code, code).astype(jnp.int32).astype(jnp.int16)


def decode(code):
    part = code.astype(jnp.float32)
    square = part * (1.0 / CODE_MAX)
    square = square * square
    square = square * square
    square = square * square * VALUE_MAX
    return jnp.where(part < 0.0, -square, square)


def live_of(owner, row, col):
    return jnp.where(owner[row, col] >= 0, 1.0, 0.0).astype(jnp.float32)


def start_loads(fields, incr, flow, F, NZ, FL, xs, ye, lsem):
    copies = []
    k = 0
    edges = []
    for side in range(2):
        for comp in range(2):
            lanes = pl.ds(128 * comp, 128)
            edges.append((fields.at[pl.ds(62 * side, 2), :, lanes], xs.at[side, comp]))
            edges.append((fields.at[:, pl.ds(120 * side, 8), lanes], ye.at[side, comp]))
    for src, dst in edges:
        copies.append(pltpu.make_async_copy(src, dst, lsem.at[k]))
        k += 1
    copies.append(pltpu.make_async_copy(flow, FL, lsem.at[k]))
    k += 1
    for comp in range(2):
        copies.append(
            pltpu.make_async_copy(
                fields.at[:, :, pl.ds(128 * comp, 128)],
                F.at[comp, pl.ds(2, NX), pl.ds(8, NY)],
                lsem.at[k],
            )
        )
        k += 1
    copies.append(pltpu.make_async_copy(incr, NZ, lsem.at[k]))
    for copy in copies:
        copy.start()
    return copies[:8], copies[8:9], copies[9:11], copies[11:]


def mask_edges(owner, xs, ye, ys):
    for side in range(2):
        for comp in range(2):
            for col in range(4):
                part = pl.ds(EDGE * col, EDGE)
                live = live_of(owner, side, col)
                for line in range(2):
                    xs[side, comp, line, part, :] = xs[side, comp, line, part, :] * live
    for side in range(2):
        for row in range(2):
            live = live_of(owner, row, 3 * side)
            for comp in range(2):
                strip = ye.at[side, comp].reshape(NX * 8, 128)
                for line in range(2):
                    for g in range(4):
                        x0 = EDGE * row + 8 * g
                        ys[side, comp, line, pl.ds(x0, 8), :] = (
                            strip[pl.ds(x0 * 8 + 6 * side + line, 8, stride=8), :] * live
                        )


def halo_copies(F, xs, ys, yr, hs, hr):
    gx, gy = lax.axis_index("gx"), lax.axis_index("gy")
    copies = []
    for side in range(2):
        step = 2 * side - 1
        tx = lax.rem(gx + step + 8, 8)
        ty = lax.rem(gy + step + 16, 16)
        copies.append(
            pltpu.make_async_remote_copy(
                xs.at[side],
                F.at[:, pl.ds(66 * (1 - side), 2), pl.ds(8, NY)],
                hs.at[side],
                hr.at[side],
                device_id=(tx, gy),
                device_id_type=MESH,
            )
        )
        copies.append(
            pltpu.make_async_remote_copy(
                ys.at[side],
                yr.at[side],
                hs.at[2 + side],
                hr.at[2 + side],
                device_id=(gx, ty),
                device_id_type=MESH,
            )
        )
    return copies


def make_coefficients(FL, CT):
    u, v = FL[0], FL[1]
    up, un = jnp.maximum(u, 0.0), jnp.minimum(u, 0.0)
    vp, vn = jnp.maximum(v, 0.0), jnp.minimum(v, 0.0)
    keep = 1.0 - 0.15 * ((up - un) + (vp - vn))
    channels = [
        keep + 0.1 * FL[2],
        0.1 * FL[3],
        0.1 * FL[4],
        keep + 0.1 * FL[5],
        0.2 * up,
        -0.2 * un,
        0.2 * vp,
        -0.2 * vn,
    ]
    for g in range(4):
        block = jnp.concatenate([c[16 * g : 16 * g + 16] for c in channels], axis=0)
        CT[g] = block.T


def mask_block(owner, F2):
    for row in range(2):
        for col in range(4):
            live = live_of(owner, row, col)

            def line(x, carry):
                part = pl.ds((2 + EDGE * row + x) * PITCH + 8 + EDGE * col, EDGE)
                for comp in range(2):
                    F2[comp, part, :] = F2[comp, part, :] * live
                return carry

            lax.fori_loop(0, EDGE, line, 0, unroll=2)


def unpack_halo(F2, yr):
    for side in range(2):
        for comp in range(2):
            for line in range(2):
                place = 6 + line if side == 1 else 136 + line
                for g in range(8):
                    F2[comp, pl.ds((2 + 8 * g) * PITCH + place, 8, stride=PITCH), :] = yr[
                        side, comp, line, pl.ds(8 * g, 8), :
                    ]


def brick_line(F2, NZ, CT, row, col, x):
    line = EDGE * row + x
    base = (2 + line) * PITCH + 8 + EDGE * col
    ys = pl.ds(pl.multiple_of(EDGE * col, EDGE), EDGE)
    table = CT[line // 16, ys, :]
    spot = jnp.full((EDGE, 128), lax.rem(line, 16), jnp.int32)
    c = [jnp.take_along_axis(table, spot + 16 * k, axis=1) for k in range(8)]
    q = [F2[comp, pl.ds(base, EDGE), :] for comp in range(2)]
    rest = jnp.maximum(20.0 - 0.8 * (q[0] * q[0] + q[1] * q[1]), 2.0)
    soft = pl.reciprocal(rest, approx=True)
    soft = soft * (2.0 - rest * soft)
    out = []
    for comp in range(2):

        def at(shift):
            return F2[comp, pl.ds(base + shift, EDGE), :]

        moved = c[4] * (at(-PITCH) - 0.25 * at(-2 * PITCH))
        moved += c[5] * (at(PITCH) - 0.25 * at(2 * PITCH))
        moved += c[6] * (at(-1) - 0.25 * at(-2))
        moved += c[7] * (at(1) - 0.25 * at(2))
        own, cross = (c[0], c[1]) if comp == 0 else (c[3], c[2])
        noise = NZ[line, ys, pl.ds(128 * comp, 128)].astype(jnp.float32)
        total = (own - soft) * q[comp] + cross * q[1 - comp] + moved + NOISE_SCALE * noise
        out.append(encode(total))
    return out


def step_kernel(
    owner, fields, incr, flow, out, F, NZ, FL, CT, xs, ye, ys, yr, codes, lsem, hs, hr, osem
):
    gx, gy = lax.axis_index("gx"), lax.axis_index("gy")
    edges, flows, block, noise = start_loads(fields, incr, flow, F, NZ, FL, xs, ye, lsem)
    barrier = pltpu.get_barrier_semaphore()
    for step in (1, -1):
        for target in (
            (lax.rem(gx + step + 8, 8), gy),
            (gx, lax.rem(gy + step + 16, 16)),
        ):
            pl.semaphore_signal(barrier, inc=1, device_id=target, device_id_type=MESH)
    for copy in edges:
        copy.wait()
    mask_edges(owner, xs, ye, ys)
    pl.semaphore_wait(barrier, 4)
    halos = halo_copies(F, xs, ys, yr, hs, hr)
    for copy in halos:
        copy.start()
    F2 = F.reshape(2, 68 * PITCH, 128)
    for copy in flows:
        copy.wait()
    make_coefficients(FL, CT)
    for copy in block:
        copy.wait()
    mask_block(owner, F2)
    for copy in noise:
        copy.wait()
    for copy in halos:
        copy.wait()
    unpack_halo(F2, yr)

    def brick(b, carry):
        row, col = b // 4, lax.rem(b, 4)

        def line(x, inner):
            coded = brick_line(F2, NZ, CT, row, col, x)
            for comp in range(2):
                codes[b, pl.ds(pl.multiple_of(x * EDGE, EDGE), EDGE), pl.ds(128 * comp, 128)] = coded[comp]
            return inner

        lax.fori_loop(0, EDGE, line, 0)
        pltpu.make_async_copy(codes.at[b], out.at[b], osem.at[b]).start()
        return carry

    lax.fori_loop(0, 8, brick, 0)
    for b in range(8):
        pltpu.make_async_copy(codes.at[b], out.at[b], osem.at[b]).wait()


def advance(fields, increments, flow_field, brick_owner):
    any_ = pl.BlockSpec(memory_space=pl.ANY)
    return pl.pallas_call(
        step_kernel,
        out_shape=jax.ShapeDtypeStruct((8, EDGE * EDGE, 256), jnp.int16),
        in_specs=[pl.BlockSpec(memory_space=pltpu.SMEM), any_, any_, any_],
        out_specs=any_,
        scratch_shapes=[
            pltpu.VMEM((2, 68, PITCH, 128), jnp.float32),
            pltpu.VMEM((NX, NY, 256), jnp.bfloat16),
            pltpu.VMEM((6, NX, NY), jnp.float32),
            pltpu.VMEM((4, 128, 128), jnp.float32),
            pltpu.VMEM((2, 2, 2, NY, 128), jnp.float32),
            pltpu.VMEM((2, 2, NX, 8, 128), jnp.float32),
            pltpu.VMEM((2, 2, 2, NX, 128), jnp.float32),
            pltpu.VMEM((2, 2, 2, NX, 128), jnp.float32),
            pltpu.VMEM((8, EDGE * EDGE, 256), jnp.int16),
            pltpu.SemaphoreType.DMA((12,)),
            pltpu.SemaphoreType.DMA((4,)),
            pltpu.SemaphoreType.DMA((4,)),
            pltpu.SemaphoreType.DMA((8,)),
        ],
        compiler_params=pltpu.CompilerParams(
            collective_id=0, has_side_effects=True, vmem_limit_bytes=56 * 2**20
        ),
    )(brick_owner, fields, increments, flow_field)


def finish_kernel(source, codes, out):
    out[0] = decode(codes[0]).reshape(out.shape[1:])


def finish(source, arrived, slots):
    return pl.pallas_call(
        finish_kernel,
        out_shape=jax.ShapeDtypeStruct((slots, EDGE, EDGE, 256), jnp.float32),
        grid_spec=pltpu.PrefetchScalarGridSpec(
            num_scalar_prefetch=1,
            grid=(slots, 2),
            in_specs=[pl.BlockSpec((1, 512, 256), lambda s, h, source: (source[s], h, 0))],
            out_specs=pl.BlockSpec((1, 16, EDGE, 256), lambda s, h, source: (s, h, 0, 0)),
        ),
        compiler_params=pltpu.CompilerParams(vmem_limit_bytes=32 * 2**20),
    )(source, arrived)


def pick_kernel(chosen, codes, out):
    out[...] = codes[...]


def pick(chosen, codes, peers):
    block = (1, EDGE * EDGE, 256)
    return pl.pallas_call(
        pick_kernel,
        out_shape=jax.ShapeDtypeStruct((peers, EDGE * EDGE, 256), jnp.int16),
        grid_spec=pltpu.PrefetchScalarGridSpec(
            num_scalar_prefetch=1,
            grid=(peers,),
            in_specs=[pl.BlockSpec(block, lambda s, chosen: (chosen[s], 0, 0))],
            out_specs=pl.BlockSpec(block, lambda s, chosen: (s, 0, 0)),
        ),
        compiler_params=pltpu.CompilerParams(vmem_limit_bytes=32 * 2**20),
    )(chosen, codes)


def on_device(fields, increments, flow_field, brick_owner):
    slot_count = 7
    peer_count = lax.axis_size("gy")
    owner_table = lax.all_gather(brick_owner, "gy", axis=1, tiled=True)
    device = lax.axis_index("gx") * peer_count + lax.axis_index("gy")
    owner_flat = brick_owner.reshape(8)
    target = jnp.where(owner_flat >= 0, owner_flat // slot_count % peer_count, -1)
    match_grid = target[None, :] == jnp.arange(peer_count, dtype=jnp.int32)[:, None]
    chosen = jnp.sum(jnp.where(match_grid, jnp.arange(8, dtype=jnp.int32)[None, :], 0), axis=1)
    wanted = device * slot_count + jnp.arange(slot_count, dtype=jnp.int32)
    column = jnp.arange(owner_table.shape[1], dtype=jnp.int32)
    found = owner_table[None, :, :] == wanted[:, None, None]
    source = jnp.sum(jnp.where(found, (column // 4)[None, None, :], 0), axis=(1, 2))
    codes = advance(fields, increments, flow_field, brick_owner)
    picked = pick(chosen, codes, peer_count)
    arrived = lax.all_to_all(picked, "gy", split_axis=0, concat_axis=0, tiled=True)
    return finish(source, arrived, slot_count)


def solution(mesh):
    in_specs = (P("gx", "gy", None), P("gx", "gy", None), P(None, "gx", "gy"), P("gx", "gy"))
    out_specs = P(("gx", "gy"), None, None, None)
    return jax.shard_map(
        on_device, mesh=mesh, in_specs=in_specs, out_specs=out_specs, check_vma=False
    )
```

time: 431 us -> 253 us (0.59)
  blocking collectives: 318 us -> 169 us
  Pallas kernels: 0 us -> 68.2 us
  other arithmetic: 64.2 us -> 1.79 us
  local copies, waits for them, and re-layouts: 29.2 us -> 5.73 us
  starting transfers between devices: 15 us -> 5.15 us
    all_gather x1, blocking collectives: 318 us -> 169 us  [on_device(): owner_table = lax.all_gather(brick_owner, 'gy', axis=1, tiled=True)]
    pallas_call x0 -> x3, Pallas kernels: none -> 68.2 us  [the longest x1 55.8 us: advance(): pl.pallas_call(step_kernel, out_shape=jax.ShapeDtypeStruct((8, EDGE * EDG...]
    gather x2 -> x0, local copies, waits for them, and re-layouts: 21.1 us -> none  [the longest x1 11.2 us: on_device(): picked = jnp.take(bricks, chosen, axis=0)]
    select_n x5 -> x1, other arithmetic: 20.4 us -> 0.01 us  [on_device(): column // 4]
    add x1 -> x0, other arithmetic: 19.1 us -> none  [stencil(): centre - TIME_STEP * transport + TIME_STEP * drift]
    sub x1 -> x0, other arithmetic: 11.1 us -> none  [stencil(): flow_parts[2][..., None] * first_part + flow_parts[3][..., None] * second]
    ppermute x4 -> x0, starting transfers between devices: 8.39 us -> none  [the longest x2 6.38 us: with_halo(): after = lax.ppermute(initial, axis, down)]
    concatenate x1 -> x0, other arithmetic: 8.1 us -> none  [with_halo(): shard = jnp.concatenate([before, shard, after], axis=dim)]
  transfers between devices with their start and end apart: 5 -> 1, of which waited for: 1 -> 0; matrix products, arithmetic and copies ran while one was open for 3% -> 0% of each run, Pallas kernels for 0% -> 0%
where the time goes in v1:
time: 253 us; the launch traced here: 250 us
  blocking collectives  169 us (67%)
  Pallas kernels  68.2 us (27%)
  local copies, waits for them, and re-layouts  5.73 us (2%)
  starting transfers between devices  5.15 us (2%)
    all_gather x1, blocking collectives, on_device(): owner_table = lax.all_gather(brick_owner, 'gy', axis=1, tiled=True)  169 us
    pallas_call x1, Pallas kernels, advance(): pl.pallas_call(step_kernel, out_shape=jax.ShapeDtypeStruct((8, EDGE * EDG...  55.8 us
    pallas_call x1, Pallas kernels, finish(): pl.pallas_call(finish_kernel, out_shape=jax.ShapeDtypeStruct((slots, EDGE...  11.2 us
    unnamed x7, local copies, waits for them, and re-layouts  5.48 us
    all_to_all x1, starting transfers between devices, on_device(): lax.all_to_all(picked, 'gy', split_axis=0, concat_axis=0, tiled=True)  5.15 us
  transfers between devices with their start and end apart: 1, of which 0 were waited for; matrix products, arithmetic and copies ran while one was open for 0% of the time, Pallas kernels for 0%

profile of v1, /device:TPU:4, one launch (start us, length us, event | category | flops | bytes accessed | tf_op | source)
XLA Modules:
  0.0 250.2 jit_solution(4831924939711611211)
XLA Ops:
  0.0 0.7 compare_and_fusion
  0.7 0.7 broadcast_divide_fusion
  1.4 0.1 and.40
  1.5 0.1 ge.11
  1.6 0.1 div.24
  1.7 0.1 select_reduce_fusion.chosen
  1.7 55.8 %shard_map.46.codes = s16[8,1024,256]{2,1,0:T(8,128)(2,1)} custom-call(s32[2,4]{1,0:T(2,128)} %owner.1, f32[64,128,256]{2,1,0:T(8,128)} %fields.1, bf16[64,128,256]{2,1,0:T(8,128)(2,1)} %incr.1, f32[6,64,128]{2,1,0:T(8,128)} %flow.1), custom_call_target="tpu_custom_call" | custom-call | tf_op jit(solution)/shard_map/pallas_call | solution.py:246
  57.5 0.0 copy-start.1
  57.5 2.2 copy-done.1
  59.7 1.3 shard_map.47
  61.0 0.0 copy-start
  61.0 3.2 %copy-done = s16[16,1024,256]{2,1,0:T(8,128)(2,1)} copy-done((s16[16,1024,256]{2,1,0:T(8,128)(2,1)}, s16[16,1024,256]{2,1,0:T(8,128)(2,1)S(1)}, u32[]{:S(2)}) %copy-start) | copy-done | bytes 8388632
  64.2 0.0 copy-start.2
  64.2 5.1 %all-to-all-start = ((s16[16,1024,256]{2,1,0:T(8,128)(2,1)}), s16[16,1024,256]{2,1,0:T(8,128)(2,1)}, u32[]{:S(2)}, u32[]{:S(2)}) async-start(s16[16,1024,256]{2,1,0:T(8,128)(2,1)} %copy-done), calls=%async_computation | async-start | bytes 16777216 | tf_op jit(solution)/shard_map/all_to_all | solution.py:324
  69.4 0.0 copy-done.2
  69.4 169.2 %all-gather = s32[16,4,2]{1,2,0:T(2,128)S(1)} all-gather(s32[1,4,2]{1,2,0:T(2,128)S(1)} %bitcast.6), channel_id=1, replica_groups=mesh['gx'=8,'gy'=16] {'gy'}, dimensions={0}, use_global_device_ids=true | all-gather | bytes 544 | tf_op jit(solution)/shard_map/all_gather | solution.py:312
  238.6 0.1 reshape.66
  238.7 0.3 fusion.source
  239.0 0.0 all-to-all-done.codes
  239.0 11.2 %shard_map.48 = f32[7,32,32,256]{3,2,1,0:T(8,128)} custom-call(s32[7]{0:T(128)S(1)} %fusion.source, s16[16,1024,256]{2,1,0:T(8,128)(2,1)} %all-to-all-done.codes), custom_call_target="tpu_custom_call" | custom-call | tf_op jit(solution)/shard_map/pallas_call | solution.py:277
  (4 shorter events, 0.0 us)
Async XLA Ops:
  57.5 2.2 copy-start.1
  61.0 3.2 %copy-start = (s16[16,1024,256]{2,1,0:T(8,128)(2,1)}, s16[16,1024,256]{2,1,0:T(8,128)(2,1)S(1)}, u32[]{:S(2)}) copy-start(s16[16,1024,256]{2,1,0:T(8,128)(2,1)S(1)} %shard_map.47) | copy-start | bytes 25165828
  64.2 5.2 %copy-start.2 = (s32[2,4]{1,0:T(2,128)S(1)}, s32[2,4]{1,0:T(2,128)}, u32[]{:S(2)}) copy-start(s32[2,4]{1,0:T(2,128)} %owner.1) | copy-start | bytes 100
  64.2 174.8 %all-to-all-start = ((s16[16,1024,256]{2,1,0:T(8,128)(2,1)}), s16[16,1024,256]{2,1,0:T(8,128)(2,1)}, u32[]{:S(2)}, u32[]{:S(2)}) async-start(s16[16,1024,256]{2,1,0:T(8,128)(2,1)} %copy-done), calls=%async_computation | async-start | bytes 16777216 | tf_op jit(solution)/shard_map/all_to_all | solution.py:324

commit v2 on v1

--- a/solution.py
+++ b/solution.py
@@ -15,6 +15,10 @@
 EDGE = 32
 PITCH = 144
 NX, NY = 64, 128
+CAPACITY = 7
+PIECES = 4
+OWN = 8 * PIECES
+ROUNDS = 25
 
 
 def encode(value):
@@ -163,13 +167,13 @@
                     ]
 
 
-def brick_line(F2, NZ, CT, row, col, x):
-    line = EDGE * row + x
+def brick_line(F2, NZ, CT, row, col, half, step):
+    line = EDGE * row + 16 * half + step
     base = (2 + line) * PITCH + 8 + EDGE * col
     ys = pl.ds(pl.multiple_of(EDGE * col, EDGE), EDGE)
-    table = CT[line // 16, ys, :]
-    spot = jnp.full((EDGE, 128), lax.rem(line, 16), jnp.int32)
-    c = [jnp.take_along_axis(table, spot + 16 * k, axis=1) for k in range(8)]
+    table = CT[2 * row + half, ys, :]
+    spots = [16 * k + step for k in range(8)]
+    c = [jnp.broadcast_to(table[:, k : k + 1], (EDGE, 128)) for k in spots]
     q = [F2[comp, pl.ds(base, EDGE), :] for comp in range(2)]
     rest = jnp.maximum(20.0 - 0.8 * (q[0] * q[0] + q[1] * q[1]), 2.0)
     soft = pl.reciprocal(rest, approx=True)
@@ -191,22 +195,117 @@
     return out
 
 
+def slot_in_pool(number):
+    return jnp.minimum(jnp.maximum(number, 0), OWN + 4 * ROUNDS - 1)
+
+
+def make_tile(owner, gy):
+    lane = lax.broadcasted_iota(jnp.int32, (8, 128), 1)
+    brick = (lane % 32) // PIECES
+    tile = jnp.zeros((8, 128), jnp.int32)
+    for b in range(8):
+        slot = jnp.maximum(owner[b // 4, b % 4], 0)
+        code = lax.rem(slot // CAPACITY, 16) * 8 + lax.rem(slot, CAPACITY) + 1
+        code = jnp.where(owner[b // 4, b % 4] >= 0, code, 0)
+        tile = jnp.where(brick == b, code, tile)
+    return jnp.where(lane // 32 == lax.rem(gy, 4), tile, 0)
+
+
+def plan_routes(tiles, plan, last, flags, gx, gy):
+    shape = (8, 512)
+    p = lax.broadcasted_iota(jnp.int32, shape, 1)
+    rowid = lax.broadcasted_iota(jnp.int32, (64, 512), 0)
+    src, brick, piece = p // 32, (p // PIECES) % 8, p % PIECES
+    code = jnp.concatenate(
+        [tiles[4 * q] + tiles[4 * q + 1] + tiles[4 * q + 2] + tiles[4 * q + 3] for q in range(4)], axis=1
+    )
+    dest, slot = (jnp.maximum(code - 1, 0)) // 8, (jnp.maximum(code - 1, 0)) % 8
+    live = code > 0
+    y, z = src // 4, src % 4
+    ty, tz = (dest // 4 - y + 4) % 4, (dest % 4 - z + 4) % 4
+    tie = (piece + brick + src) % 2
+    kz = jnp.where(tz == 2, tie, jnp.where(tz == 3, 1, 0))
+    ky = jnp.where(ty == 2, tie, jnp.where(ty == 3, 1, 0))
+    nz = jnp.where(live, jnp.where(tz == 3, 1, tz), 0)
+    ny = jnp.where(live, jnp.where(ty == 3, 1, ty), 0)
+    first = (piece // 2 + brick) % 2
+    lane = lax.broadcasted_iota(jnp.int32, (8, 128), 1)
+    mine = lax.rem(rowid[:, :1], 16) == gy
+
+    def step(r, carry):
+        nz, ny, y, z, loc, ready = carry
+        usez = jnp.logical_and(nz > 0, jnp.logical_or(first == 0, ny == 0))
+        dist = nz + ny
+        active = jnp.logical_and(dist > 0, ready <= r)
+        k = jnp.where(usez, kz, ky + 2)
+        key = jnp.where(active, k * 16 + y * 4 + z, -1)
+        score = dist * 512 + loc + 1
+        key = jnp.concatenate([key] * 8, axis=0)
+        wide = jnp.concatenate([score] * 8, axis=0)
+        bids = jnp.where(rowid == key, wide, 0)
+        best = jnp.maximum(jnp.max(bids, axis=1, keepdims=True), 1)
+        won = jnp.where(bids == best, 1, 0)
+        moved = won[0:8]
+        for i in range(1, 8):
+            moved = jnp.maximum(moved, won[8 * i : 8 * i + 8])
+        moved = jnp.broadcast_to(jnp.max(moved, axis=0, keepdims=True), shape) > 0
+        own = jnp.where(mine, best, 0)
+        line = jnp.zeros((8, 128), jnp.int32)
+        for i in range(4):
+            pick = jnp.max(own[16 * i : 16 * i + 16], axis=0, keepdims=True)
+            line = jnp.where(lane == i, jnp.broadcast_to(pick, (8, 128)), line)
+        number = jnp.maximum(line - 1, 0) % 512
+        plan[pl.ds(pl.multiple_of(8 * r, 8), 8), :] = number
+        wentz = jnp.logical_and(moved, usez)
+        wenty = jnp.logical_and(moved, jnp.logical_not(usez))
+        nz = jnp.where(wentz, nz - 1, nz)
+        ny = jnp.where(wenty, ny - 1, ny)
+        z = jnp.where(wentz, (z + 5 - 2 * kz) % 4, z)
+        y = jnp.where(wenty, (y + 5 - 2 * ky) % 4, y)
+        loc = jnp.where(moved, OWN + 4 * r + k, loc)
+        ready = jnp.where(moved, r + 2, ready)
+        return nz, ny, y, z, loc, ready
+
+    start = (nz, ny, y, z, brick * PIECES + piece, brick)
+    nz, ny, y, z, loc, ready = lax.fori_loop(0, ROUNDS, step, start)
+    row = lax.broadcasted_iota(jnp.int32, shape, 0)
+    wanted = jnp.logical_and(live, jnp.logical_and(dest == gy, slot == row))
+    for i in range(PIECES):
+        found = jnp.where(jnp.logical_and(wanted, piece == i), loc, 0)
+        found = jnp.max(found, axis=1, keepdims=True)
+        last[8 * i : 8 * i + 8, :] = jnp.broadcast_to(found, (8, 128))
+    left = jnp.max(nz + ny, axis=1, keepdims=True)
+    flags[gx] = jnp.broadcast_to(left, (8, 128))
+
+
 def step_kernel(
-    owner, fields, incr, flow, out, F, NZ, FL, CT, xs, ye, ys, yr, codes, lsem, hs, hr, osem
+    owner, fields, incr, flow, mailed, own_codes, unfinished, F, NZ, FL, CT, xs, ye, ys, yr, pool, landing, leaving,
+    shelf, tiles, plan, last, flags, plan_s, last_s, lsem, hs, hr, tsend, trecv, fsend, frecv, msem, ssem, rsem, osem,
 ):
     gx, gy = lax.axis_index("gx"), lax.axis_index("gy")
     edges, flows, block, noise = start_loads(fields, incr, flow, F, NZ, FL, xs, ye, lsem)
     barrier = pltpu.get_barrier_semaphore()
-    for step in (1, -1):
-        for target in (
-            (lax.rem(gx + step + 8, 8), gy),
-            (gx, lax.rem(gy + step + 16, 16)),
-        ):
-            pl.semaphore_signal(barrier, inc=1, device_id=target, device_id_type=MESH)
+    row_peers = [lax.rem(gy + i, 16) for i in range(1, 16)]
+    col_peers = [lax.rem(gx + i, 8) for i in range(1, 8)]
+    for peer in row_peers:
+        pl.semaphore_signal(barrier, inc=1, device_id=(gx, peer), device_id_type=MESH)
+    for peer in col_peers:
+        pl.semaphore_signal(barrier, inc=1, device_id=(peer, gy), device_id_type=MESH)
+    tiles[gy] = make_tile(owner, gy)
     for copy in edges:
         copy.wait()
     mask_edges(owner, xs, ye, ys)
-    pl.semaphore_wait(barrier, 4)
+    pl.semaphore_wait(barrier, 22)
+    mail = []
+    for i, peer in enumerate(row_peers):
+        mail.append(
+            pltpu.make_async_remote_copy(
+                tiles.at[gy], tiles.at[gy], tsend.at[i], trecv.at[i],
+                device_id=(gx, peer), device_id_type=MESH,
+            )
+        )
+    for copy in mail:
+        copy.start()
     halos = halo_copies(F, xs, ys, yr, hs, hr)
     for copy in halos:
         copy.start()
@@ -217,37 +316,128 @@
     for copy in block:
         copy.wait()
     mask_block(owner, F2)
+    for copy in mail:
+        copy.wait()
+    plan_routes(tiles, plan, last, flags, gx, gy)
+    news = [
+        pltpu.make_async_remote_copy(
+            flags.at[gx], flags.at[gx], fsend.at[i], frecv.at[i],
+            device_id=(peer, gy), device_id_type=MESH,
+        )
+        for i, peer in enumerate(col_peers)
+    ]
+    for copy in news:
+        copy.start()
+    scalars = [
+        pltpu.make_async_copy(plan, plan_s, msem.at[0]),
+        pltpu.make_async_copy(last, last_s, msem.at[1]),
+    ]
+    for copy in scalars:
+        copy.start()
     for copy in noise:
         copy.wait()
     for copy in halos:
         copy.wait()
     unpack_halo(F2, yr)
 
-    def brick(b, carry):
+    def brick(b):
         row, col = b // 4, lax.rem(b, 4)
 
-        def line(x, inner):
-            coded = brick_line(F2, NZ, CT, row, col, x)
-            for comp in range(2):
-                codes[b, pl.ds(pl.multiple_of(x * EDGE, EDGE), EDGE), pl.ds(128 * comp, 128)] = coded[comp]
-            return inner
-
-        lax.fori_loop(0, EDGE, line, 0)
-        pltpu.make_async_copy(codes.at[b], out.at[b], osem.at[b]).start()
+        def lines(half, carry):
+            for step in range(16):
+                coded = brick_line(F2, NZ, CT, row, col, half, step)
+                for comp in range(2):
+                    place = (PIECES * b + 2 * half + step // 8, pl.ds(32 * (step % 8), 32), pl.ds(128 * comp, 128))
+                    pool[place] = coded[comp]
+            return carry
+
+        lax.fori_loop(0, 2, lines, 0)
+
+    y, z = gy // 4, lax.rem(gy, 4)
+    targets = [
+        4 * y + lax.rem(z + 1, 4),
+        4 * y + lax.rem(z + 3, 4),
+        4 * lax.rem(y + 1, 4) + z,
+        4 * lax.rem(y + 3, 4) + z,
+    ]
+
+    def hop(r, k):
+        side = lax.rem(r, 2)
+        return pltpu.make_async_remote_copy(
+            leaving.at[side, k], landing.at[r, k], ssem.at[side, k], rsem.at[r, k],
+            device_id=(gx, targets[k]), device_id_type=MESH,
+        )
+
+    def collect(r):
+        for k in range(4):
+            copy = hop(r, k)
+            copy.wait()
+            pool[OWN + 4 * r + k] = landing[r, k]
+
+    def send(r):
+        side = lax.rem(r, 2)
+        for k in range(4):
+            leaving[side, k] = pool[slot_in_pool(plan_s[8 * r, k])]
+            hop(r, k).start()
+
+    brick(0)
+    for copy in scalars:
+        copy.wait()
+    send(0)
+    brick(1)
+    send(1)
+
+    def early(r, carry):
+        brick(r)
+        collect(r - 2)
+        send(r)
         return carry
 
-    lax.fori_loop(0, 8, brick, 0)
-    for b in range(8):
-        pltpu.make_async_copy(codes.at[b], out.at[b], osem.at[b]).wait()
+    lax.fori_loop(2, 8, early, 0)
+    keep = pltpu.make_async_copy(pool.at[pl.ds(0, OWN)], own_codes, msem.at[2])
+    keep.start()
+
+    def later(r, carry):
+        collect(r - 2)
+        send(r)
+        return carry
+
+    lax.fori_loop(8, ROUNDS, later, 0)
+    collect(ROUNDS - 2)
+    collect(ROUNDS - 1)
+
+    def deliver(s, carry):
+        for i in range(PIECES):
+            shelf[PIECES * s + i] = pool[slot_in_pool(last_s[8 * i + s, 0])]
+        part = pl.ds(PIECES * s, PIECES)
+        pltpu.make_async_copy(shelf.at[part], mailed.at[part], osem.at[s]).start()
+        return carry
+
+    lax.fori_loop(0, CAPACITY, deliver, 0)
+    for copy in news:
+        copy.wait()
+    tell = pltpu.make_async_copy(flags, unfinished, msem.at[3])
+    tell.start()
+    for s in range(CAPACITY):
+        part = pl.ds(PIECES * s, PIECES)
+        pltpu.make_async_copy(shelf.at[part], mailed.at[part], osem.at[s]).wait()
+    keep.wait()
+    tell.wait()
 
 
 def advance(fields, increments, flow_field, brick_owner):
     any_ = pl.BlockSpec(memory_space=pl.ANY)
+    packet = (EDGE * EDGE // PIECES, 256)
+    dma = pltpu.SemaphoreType.DMA
     return pl.pallas_call(
         step_kernel,
-        out_shape=jax.ShapeDtypeStruct((8, EDGE * EDGE, 256), jnp.int16),
+        out_shape=(
+            jax.ShapeDtypeStruct((CAPACITY * PIECES, *packet), jnp.int16),
+            jax.ShapeDtypeStruct((OWN, *packet), jnp.int16),
+            jax.ShapeDtypeStruct((8, 8, 128), jnp.int32),
+        ),
         in_specs=[pl.BlockSpec(memory_space=pltpu.SMEM), any_, any_, any_],
-        out_specs=any_,
+        out_specs=(any_, any_, any_),
         scratch_shapes=[
             pltpu.VMEM((2, 68, PITCH, 128), jnp.float32),
             pltpu.VMEM((NX, NY, 256), jnp.bfloat16),
@@ -257,14 +447,30 @@
             pltpu.VMEM((2, 2, NX, 8, 128), jnp.float32),
             pltpu.VMEM((2, 2, 2, NX, 128), jnp.float32),
             pltpu.VMEM((2, 2, 2, NX, 128), jnp.float32),
-            pltpu.VMEM((8, EDGE * EDGE, 256), jnp.int16),
-            pltpu.SemaphoreType.DMA((12,)),
-            pltpu.SemaphoreType.DMA((4,)),
-            pltpu.SemaphoreType.DMA((4,)),
-            pltpu.SemaphoreType.DMA((8,)),
+            pltpu.VMEM((OWN + 4 * ROUNDS, *packet), jnp.int16),
+            pltpu.VMEM((ROUNDS, 4, *packet), jnp.int16),
+            pltpu.VMEM((2, 4, *packet), jnp.int16),
+            pltpu.VMEM((CAPACITY * PIECES, *packet), jnp.int16),
+            pltpu.VMEM((16, 8, 128), jnp.int32),
+            pltpu.VMEM((8 * ROUNDS, 128), jnp.int32),
+            pltpu.VMEM((8 * PIECES, 128), jnp.int32),
+            pltpu.VMEM((8, 8, 128), jnp.int32),
+            pltpu.SMEM((8 * ROUNDS, 128), jnp.int32),
+            pltpu.SMEM((8 * PIECES, 128), jnp.int32),
+            dma((12,)),
+            dma((4,)),
+            dma((4,)),
+            dma((15,)),
+            dma((15,)),
+            dma((7,)),
+            dma((7,)),
+            dma((4,)),
+            dma((2, 4)),
+            dma((ROUNDS, 4)),
+            dma((CAPACITY,)),
         ],
         compiler_params=pltpu.CompilerParams(
-            collective_id=0, has_side_effects=True, vmem_limit_bytes=56 * 2**20
+            collective_id=0, has_side_effects=True, vmem_limit_bytes=58 * 2**20
         ),
     )(brick_owner, fields, increments, flow_field)
 
@@ -306,23 +512,33 @@
     )(chosen, codes)
 
 
-def on_device(fields, increments, flow_field, brick_owner):
-    slot_count = 7
+def dense(codes, owner_table, brick_owner):
     peer_count = lax.axis_size("gy")
-    owner_table = lax.all_gather(brick_owner, "gy", axis=1, tiled=True)
     device = lax.axis_index("gx") * peer_count + lax.axis_index("gy")
     owner_flat = brick_owner.reshape(8)
-    target = jnp.where(owner_flat >= 0, owner_flat // slot_count % peer_count, -1)
+    target = jnp.where(owner_flat >= 0, owner_flat // CAPACITY % peer_count, -1)
     match_grid = target[None, :] == jnp.arange(peer_count, dtype=jnp.int32)[:, None]
     chosen = jnp.sum(jnp.where(match_grid, jnp.arange(8, dtype=jnp.int32)[None, :], 0), axis=1)
-    wanted = device * slot_count + jnp.arange(slot_count, dtype=jnp.int32)
+    wanted = device * CAPACITY + jnp.arange(CAPACITY, dtype=jnp.int32)
     column = jnp.arange(owner_table.shape[1], dtype=jnp.int32)
     found = owner_table[None, :, :] == wanted[:, None, None]
     source = jnp.sum(jnp.where(found, (column // 4)[None, None, :], 0), axis=(1, 2))
-    codes = advance(fields, increments, flow_field, brick_owner)
-    picked = pick(chosen, codes, peer_count)
+    picked = pick(chosen, codes.reshape(8, EDGE * EDGE, 256), peer_count)
     arrived = lax.all_to_all(picked, "gy", split_axis=0, concat_axis=0, tiled=True)
-    return finish(source, arrived, slot_count)
+    return finish(source, arrived, CAPACITY)
+
+
+def on_device(fields, increments, flow_field, brick_owner):
+    mailed, codes, unfinished = advance(fields, increments, flow_field, brick_owner)
+
+    def routed():
+        return decode(mailed.reshape(CAPACITY, EDGE, EDGE, 256))
+
+    def fallback():
+        owner_table = lax.all_gather(brick_owner, "gy", axis=1, tiled=True)
+        return dense(codes, owner_table, brick_owner)
+
+    return lax.cond(jnp.max(unfinished) == 0, routed, fallback)
 
 
 def solution(mesh):

time: 253 us -> 113 us (0.45)
  blocking collectives: 169 us -> 0 us
  Pallas kernels: 68.2 us -> 98.7 us
  other arithmetic: 1.79 us -> 9.54 us
  starting transfers between devices: 5.15 us -> 0 us
  local copies, waits for them, and re-layouts: 5.73 us -> 3.05 us
    all_gather x1 -> x0, blocking collectives: 169 us -> none  [on_device(): owner_table = lax.all_gather(brick_owner, 'gy', axis=1, tiled=True)]
    pallas_call x3 -> x1, Pallas kernels: 68.2 us -> 98.7 us  [advance(): pl.pallas_call(step_kernel, out_shape=(jax.ShapeDtypeStruct((CAPACITY * P...]
    all_to_all x1 -> x0, starting transfers between devices: 5.15 us -> none  [on_device(): lax.all_to_all(picked, 'gy', split_axis=0, concat_axis=0, tiled=True)]
    mul x0 -> x1, other arithmetic: none -> 4.32 us  [decode(): square = square * square * VALUE_MAX]
    unnamed x7 -> x4, local copies, waits for them, and re-layouts: 5.48 us -> 3.05 us
  transfers between devices with their start and end apart: 1 -> 0, of which waited for: 0 -> 0; matrix products, arithmetic and copies ran while one was open for 0% -> 0% of each run, Pallas kernels for 0% -> 0%
where the time goes in v2:
time: 113 us; the launch traced here: 112 us
  Pallas kernels  98.7 us (87%)
  other arithmetic  9.54 us (8%)
  local copies, waits for them, and re-layouts  3.05 us (3%)
    pallas_call x1, Pallas kernels, advance(): pl.pallas_call(step_kernel, out_shape=(jax.ShapeDtypeStruct((CAPACITY * P...  98.7 us
    mul x1, other arithmetic, decode(): square = square * square * VALUE_MAX  4.32 us
    unnamed x4, local copies, waits for them, and re-layouts  3.05 us

profile of v2, /device:TPU:4, one launch (start us, length us, event | category | flops | bytes accessed | tf_op | source)
XLA Modules:
  0.0 112.0 jit_solution(6360108161917573805)
XLA Ops:
  0.0 0.0 copy-start.3
  0.0 98.7 %shard_map.48 = (s16[28,256,256]{2,1,0:T(8,128)(2,1)}, s16[32,256,256]{2,1,0:T(8,128)(2,1)}, s32[8,8,128]{2,1,0:T(8,128)}) custom-call(s32[2,4]{1,0:T(2,128)} %owner.1, f32[64,128,256]{2,1,0:T(8,128)} %fields.1, bf16[64,128,256]{2,1,0:T(8,128)(2,1)} %incr.1, f32[6,64,128]{2,1,0:T(8,128)} %flow.1), custom_call_target="tpu_custom_call" | custom-call | tf_op jit(solution)/shard_map/pallas_call | solution.py:432
  98.7 1.4 %reduce_max.9 = s32[]{:T(128)} reduce(s32[8,8,128]{2,1,0:T(8,128)} %get-tuple-element.18, s32[]{:T(128)} %constant.60.clone.1), dimensions={0,1,2}, to_apply=%region_0.0 | reduce | flops 8191 | bytes 32776 | tf_op jit(solution)/shard_map/reduce_max | solution.py:541
  100.7 0.0 copy-done.3
  100.7 8.2 %conditional.1 = (f32[7,32,32,256]{3,2,1,0:T(8,128)S(1)}) conditional(s32[]{:T(128)} %convert_element_type.7, (s32[2,4]{1,0:T(2,128)S(1)}, s16[32,256,256]{2,1,0:T(8,128)(2,1)}) %tuple.18, s16[28,256,256]{2,1,0:T(8,128)(2,1)} %get-tuple-element.20), branch_computations={%region_1.4_spmd, %region_4.5_spmd} | conditional | flops 18350080 | bytes 58724500 | solution.py:541
  100.8 0.0 copy-start.1
  100.8 4.3 %fusion.6 = f32[28,256,256]{2,1,0:T(8,128)S(1)} fusion(s16[28,256,256]{2,1,0:T(8,128)(2,1)} %param.1), kind=kLoop, calls=%fused_computation.24 | loop fusion | flops 11010048 | bytes 11010048 | tf_op jit(solution)/shard_map/cond/branch_1_fun/mul | solution.py:37
  105.1 0.0 copy-done.1
  105.1 1.9 %convert_compare_fusion = pred[28,256,256]{2,1,0:T(8,128)(4,1)S(1)} fusion(s16[28,256,256]{2,1,0:T(8,128)(2,1)S(1)} %copy-done.1), kind=kLoop, calls=%fused_computation.20 | loop fusion | flops 3670016 | bytes 5505024 | tf_op jit(solution)/shard_map/cond/branch_1_fun/lt | solution.py:38
  107.0 1.9 %negate_select_fusion = f32[7,32,32,256]{3,2,1,0:T(8,128)S(1)} fusion(pred[7,32,32,256]{3,2,1,0:T(8,128)(4,1)S(1)} %bitcast.10, f32[7,32,32,256]{3,2,1,0:T(8,128)S(1)} %bitcast.9), kind=kLoop, calls=%fused_computation.18 | loop fusion | flops 3670016 | bytes 16515072 | tf_op jit(solution)/shard_map/cond/branch_1_fun/jit(_where)/select_n | solution.py:38
  108.9 0.0 copy-start.2
  108.9 3.0 %copy-done.2 = f32[7,32,32,256]{3,2,1,0:T(8,128)} copy-done((f32[7,32,32,256]{3,2,1,0:T(8,128)}, f32[7,32,32,256]{3,2,1,0:T(8,128)S(1)}, u32[]{:S(2)}) %copy-start.2) | copy-done | bytes 7340056
Async XLA Ops:
  0.0 100.7 %copy-start.3 = (s32[2,4]{1,0:T(2,128)S(1)}, s32[2,4]{1,0:T(2,128)}, u32[]{:S(2)}) copy-start(s32[2,4]{1,0:T(2,128)} %owner.1) | copy-start | bytes 100
  100.8 4.3 %copy-start.1 = (s16[28,256,256]{2,1,0:T(8,128)(2,1)S(1)}, s16[28,256,256]{2,1,0:T(8,128)(2,1)}, u32[]{:S(2)}) copy-start(s16[28,256,256]{2,1,0:T(8,128)(2,1)} %param.1) | copy-start | bytes 11010052 | tf_op jit(solution)/shard_map/cond
  108.9 3.1 %copy-start.2 = (f32[7,32,32,256]{3,2,1,0:T(8,128)}, f32[7,32,32,256]{3,2,1,0:T(8,128)S(1)}, u32[]{:S(2)}) copy-start(f32[7,32,32,256]{3,2,1,0:T(8,128)S(1)} %get-tuple-element.28) | copy-start | bytes 22020100

commit v3 on v2

--- a/solution.py
+++ b/solution.py
@@ -18,7 +18,9 @@
 CAPACITY = 7
 PIECES = 4
 OWN = 8 * PIECES
-ROUNDS = 25
+ROUNDS = 21
+DELAY = 2
+SEARCH = 2
 
 
 def encode(value):
@@ -211,76 +213,143 @@
     return jnp.where(lane // 32 == lax.rem(gy, 4), tile, 0)
 
 
-def plan_routes(tiles, plan, last, flags, gx, gy):
-    shape = (8, 512)
-    p = lax.broadcasted_iota(jnp.int32, shape, 1)
-    rowid = lax.broadcasted_iota(jnp.int32, (64, 512), 0)
-    src, brick, piece = p // 32, (p // PIECES) % 8, p % PIECES
+NZ_, NY_, Z_, Y_, KZ_, KY_, FIRST_, LOC_, READY_ = range(9)
+STATE = (8, 512)
+
+
+def lanes_of():
+    p = lax.broadcasted_iota(jnp.int32, STATE, 1)
+    return p // 32, (p // PIECES) % 8, p % PIECES
+
+
+def decode_tiles(tiles):
     code = jnp.concatenate(
         [tiles[4 * q] + tiles[4 * q + 1] + tiles[4 * q + 2] + tiles[4 * q + 3] for q in range(4)], axis=1
     )
-    dest, slot = (jnp.maximum(code - 1, 0)) // 8, (jnp.maximum(code - 1, 0)) % 8
-    live = code > 0
+    number = jnp.maximum(code - 1, 0)
+    return code > 0, number // 8, number % 8
+
+
+def open_plan(tiles, st):
+    src, brick, piece = lanes_of()
+    live, dest, _ = decode_tiles(tiles)
     y, z = src // 4, src % 4
-    ty, tz = (dest // 4 - y + 4) % 4, (dest % 4 - z + 4) % 4
-    tie = (piece + brick + src) % 2
-    kz = jnp.where(tz == 2, tie, jnp.where(tz == 3, 1, 0))
-    ky = jnp.where(ty == 2, tie, jnp.where(ty == 3, 1, 0))
-    nz = jnp.where(live, jnp.where(tz == 3, 1, tz), 0)
-    ny = jnp.where(live, jnp.where(ty == 3, 1, ty), 0)
-    first = (piece // 2 + brick) % 2
+    ty, tz = (dest // 4 - y) & 3, (dest % 4 - z) & 3
+    tie = (piece + brick + src) & 1
+    st[NZ_] = jnp.where(live, jnp.where(tz == 3, 1, tz), 0)
+    st[NY_] = jnp.where(live, jnp.where(ty == 3, 1, ty), 0)
+    st[Z_] = z
+    st[Y_] = y
+    st[KZ_] = jnp.where(tz == 2, tie, jnp.where(tz == 3, 1, 0))
+    st[KY_] = jnp.where(ty == 2, tie, jnp.where(ty == 3, 1, 0))
+    st[FIRST_] = (piece // 2 + brick) & 1
+    st[LOC_] = brick * PIECES + piece
+    st[READY_] = jnp.maximum(brick - 1, 0)
+
+
+def balance(st, t):
+    nz, ny, z, y = st[NZ_], st[NY_], st[Z_], st[Y_]
+    kz, ky, first = st[KZ_], st[KY_], st[FIRST_]
+    kind = lax.rem(t, 3)
+    one = [jnp.where(kind == i, 1, 0) for i in range(3)]
+    flip0 = one[0] * jnp.minimum(nz, 1) * jnp.minimum(ny, 1)
+    flip1 = one[1] * (nz >> 1)
+    flip2 = one[2] * (ny >> 1)
+    row = lax.broadcasted_iota(jnp.int32, STATE, 0)
+    other, j = row >> 2, row & 3
+    f = first ^ (flip0 * other)
+    lz = kz ^ (flip1 * other)
+    ly = ky ^ (flip2 * other)
+    zfirst = f == 0
+    onz = jnp.where(zfirst, jnp.where(j < nz, 1, 0), jnp.where(j >= ny, 1, 0))
+    zc = jnp.where(zfirst, jnp.minimum(j, nz), jnp.maximum(j - ny, 0))
+    yc = jnp.where(zfirst, jnp.maximum(j - nz, 0), jnp.minimum(j, ny))
+    zz = (z + (1 - 2 * lz) * zc) & 3
+    yy = (y + (1 - 2 * ly) * yc) & 3
+    link = jnp.where(onz == 1, lz, ly + 2) * 16 + yy * 4 + zz
+    used = j < nz + ny
+    link = jnp.where(used, link, 64)
+    rowid = lax.broadcasted_iota(jnp.int32, (64, 512), 0)
+    count = jnp.zeros((64, 512), jnp.int32)
+    for i in range(4):
+        here = jnp.broadcast_to(link[i : i + 1], (64, 512))
+        count = count + jnp.where(rowid == here, 1, 0)
+    count = count[:, :128] + count[:, 128:256] + count[:, 256:384] + count[:, 384:]
+    count = jnp.broadcast_to(jnp.sum(count, axis=1, keepdims=True), (64, 128))
+    diagonal = lax.broadcasted_iota(jnp.int32, (64, 128), 0) == lax.broadcasted_iota(jnp.int32, (64, 128), 1)
+    count = jnp.where(diagonal, count, 0)
+    load = count[0:8]
+    for i in range(1, 8):
+        load = load + count[8 * i : 8 * i + 8]
+    load = jnp.broadcast_to(jnp.sum(load, axis=0, keepdims=True), (8, 128))
+    there = jnp.concatenate(
+        [jnp.take_along_axis(load, link[:, 128 * q : 128 * q + 128], axis=1) for q in range(4)], axis=1
+    )
+    shared = one[1] * (1 - onz) + one[2] * onz
+    there = there + other * (1 - shared)
+    cost = jnp.where(used, there * there, 0) * (2 * other - 1)
+    gain = jnp.broadcast_to(jnp.sum(cost, axis=0, keepdims=True), STATE)
+    p = lax.broadcasted_iota(jnp.int32, STATE, 1)
+    turn = ((p * 7 + (p >> 5) * 3 + t // 3) & 3) == 0
+    go = jnp.where(jnp.logical_and(gain < 0, turn), 1, 0)
+    st[FIRST_] = first ^ (flip0 * go)
+    st[KZ_] = kz ^ (flip1 * go)
+    st[KY_] = ky ^ (flip2 * go)
+
+
+def plan_round(st, plan, r, gy):
+    nz, ny, z, y = st[NZ_], st[NY_], st[Z_], st[Y_]
+    kz, ky, loc, ready = st[KZ_], st[KY_], st[LOC_], st[READY_]
+    rowid = lax.broadcasted_iota(jnp.int32, (64, 512), 0)
     lane = lax.broadcasted_iota(jnp.int32, (8, 128), 1)
-    mine = lax.rem(rowid[:, :1], 16) == gy
-
-    def step(r, carry):
-        nz, ny, y, z, loc, ready = carry
-        usez = jnp.logical_and(nz > 0, jnp.logical_or(first == 0, ny == 0))
-        dist = nz + ny
-        active = jnp.logical_and(dist > 0, ready <= r)
-        k = jnp.where(usez, kz, ky + 2)
-        key = jnp.where(active, k * 16 + y * 4 + z, -1)
-        score = dist * 512 + loc + 1
-        key = jnp.concatenate([key] * 8, axis=0)
-        wide = jnp.concatenate([score] * 8, axis=0)
-        bids = jnp.where(rowid == key, wide, 0)
-        best = jnp.maximum(jnp.max(bids, axis=1, keepdims=True), 1)
-        won = jnp.where(bids == best, 1, 0)
-        moved = won[0:8]
-        for i in range(1, 8):
-            moved = jnp.maximum(moved, won[8 * i : 8 * i + 8])
-        moved = jnp.broadcast_to(jnp.max(moved, axis=0, keepdims=True), shape) > 0
-        own = jnp.where(mine, best, 0)
-        line = jnp.zeros((8, 128), jnp.int32)
-        for i in range(4):
-            pick = jnp.max(own[16 * i : 16 * i + 16], axis=0, keepdims=True)
-            line = jnp.where(lane == i, jnp.broadcast_to(pick, (8, 128)), line)
-        number = jnp.maximum(line - 1, 0) % 512
-        plan[pl.ds(pl.multiple_of(8 * r, 8), 8), :] = number
-        wentz = jnp.logical_and(moved, usez)
-        wenty = jnp.logical_and(moved, jnp.logical_not(usez))
-        nz = jnp.where(wentz, nz - 1, nz)
-        ny = jnp.where(wenty, ny - 1, ny)
-        z = jnp.where(wentz, (z + 5 - 2 * kz) % 4, z)
-        y = jnp.where(wenty, (y + 5 - 2 * ky) % 4, y)
-        loc = jnp.where(moved, OWN + 4 * r + k, loc)
-        ready = jnp.where(moved, r + 2, ready)
-        return nz, ny, y, z, loc, ready
-
-    start = (nz, ny, y, z, brick * PIECES + piece, brick)
-    nz, ny, y, z, loc, ready = lax.fori_loop(0, ROUNDS, step, start)
-    row = lax.broadcasted_iota(jnp.int32, shape, 0)
+    mine = (rowid[:, :1] & 15) == gy
+    usez = jnp.logical_and(nz > 0, jnp.logical_or(st[FIRST_] == 0, ny == 0))
+    dist = nz + ny
+    active = jnp.logical_and(dist > 0, ready <= r)
+    k = jnp.where(usez, kz, ky + 2)
+    key = jnp.where(active, k * 16 + y * 4 + z, -1)
+    score = dist * 512 + loc + 1
+    key = jnp.concatenate([key] * 8, axis=0)
+    wide = jnp.concatenate([score] * 8, axis=0)
+    bids = jnp.where(rowid == key, wide, 0)
+    best = jnp.maximum(jnp.max(bids, axis=1, keepdims=True), 1)
+    won = jnp.where(bids == best, 1, 0)
+    moved = won[0:8]
+    for i in range(1, 8):
+        moved = jnp.maximum(moved, won[8 * i : 8 * i + 8])
+    moved = jnp.broadcast_to(jnp.max(moved, axis=0, keepdims=True), STATE)
+    own = jnp.where(mine, best, 0)
+    line = jnp.zeros((8, 128), jnp.int32)
+    for i in range(4):
+        chosen = jnp.max(own[16 * i : 16 * i + 16], axis=0, keepdims=True)
+        line = jnp.where(lane == i, jnp.broadcast_to(chosen, (8, 128)), line)
+    plan[r] = jnp.maximum(line - 1, 0) & 511
+    wentz = jnp.where(usez, moved, 0)
+    wenty = moved - wentz
+    st[NZ_] = nz - wentz
+    st[NY_] = ny - wenty
+    st[Z_] = (z + wentz * (1 - 2 * kz)) & 3
+    st[Y_] = (y + wenty * (1 - 2 * ky)) & 3
+    st[LOC_] = jnp.where(moved == 1, OWN + 4 * r + k, loc)
+    st[READY_] = jnp.where(moved == 1, r + 1 + DELAY, ready)
+
+
+def close_plan(tiles, st, last, flags, gx, gy):
+    _, _, piece = lanes_of()
+    live, dest, slot = decode_tiles(tiles)
+    row = lax.broadcasted_iota(jnp.int32, STATE, 0)
     wanted = jnp.logical_and(live, jnp.logical_and(dest == gy, slot == row))
     for i in range(PIECES):
-        found = jnp.where(jnp.logical_and(wanted, piece == i), loc, 0)
-        found = jnp.max(found, axis=1, keepdims=True)
-        last[8 * i : 8 * i + 8, :] = jnp.broadcast_to(found, (8, 128))
-    left = jnp.max(nz + ny, axis=1, keepdims=True)
+        found = jnp.where(jnp.logical_and(wanted, piece == i), st[LOC_], 0)
+        last[8 * i : 8 * i + 8, :] = jnp.broadcast_to(jnp.max(found, axis=1, keepdims=True), (8, 128))
+    left = jnp.max(st[NZ_] + st[NY_], axis=1, keepdims=True)
     flags[gx] = jnp.broadcast_to(left, (8, 128))
 
 
 def step_kernel(
     owner, fields, incr, flow, mailed, own_codes, unfinished, F, NZ, FL, CT, xs, ye, ys, yr, pool, landing, leaving,
-    shelf, tiles, plan, last, flags, plan_s, last_s, lsem, hs, hr, tsend, trecv, fsend, frecv, msem, ssem, rsem, osem,
+    shelf, tiles, st, plan, last, flags, plan_s, last_s, flags_s,
+    lsem, hs, hr, tsend, trecv, fsend, frecv, msem, psem, ssem, rsem, osem,
 ):
     gx, gy = lax.axis_index("gx"), lax.axis_index("gy")
     edges, flows, block, noise = start_loads(fields, incr, flow, F, NZ, FL, xs, ye, lsem)
@@ -318,7 +387,102 @@
     mask_block(owner, F2)
     for copy in mail:
         copy.wait()
-    plan_routes(tiles, plan, last, flags, gx, gy)
+    open_plan(tiles, st)
+
+    def search(t, carry):
+        balance(st, t)
+        return carry
+
+    lax.fori_loop(0, 6, search, 0)
+
+    def row_copy(r):
+        return pltpu.make_async_copy(plan.at[r], plan_s.at[r], psem.at[r])
+
+    plan_round(st, plan, 0, gy)
+    row_copy(0).start()
+    for copy in noise:
+        copy.wait()
+    for copy in halos:
+        copy.wait()
+    unpack_halo(F2, yr)
+
+    def brick(b):
+        row, col = b // 4, lax.rem(b, 4)
+
+        def lines(half, carry):
+            for step in range(16):
+                coded = brick_line(F2, NZ, CT, row, col, half, step)
+                for comp in range(2):
+                    place = (PIECES * b + 2 * half + step // 8, pl.ds(32 * (step % 8), 32), pl.ds(128 * comp, 128))
+                    pool[place] = coded[comp]
+            return carry
+
+        lax.fori_loop(0, 2, lines, 0)
+
+    y, z = gy // 4, lax.rem(gy, 4)
+    targets = [
+        4 * y + lax.rem(z + 1, 4),
+        4 * y + lax.rem(z + 3, 4),
+        4 * lax.rem(y + 1, 4) + z,
+        4 * lax.rem(y + 3, 4) + z,
+    ]
+
+    def hop(r, k):
+        side = lax.rem(r, DELAY + 1)
+        return pltpu.make_async_remote_copy(
+            leaving.at[side, k], landing.at[r, k], ssem.at[side, k], rsem.at[r, k],
+            device_id=(gx, targets[k]), device_id_type=MESH,
+        )
+
+    def collect(r):
+        for k in range(4):
+            copy = hop(r, k)
+            copy.wait()
+            pool[OWN + 4 * r + k] = landing[r, k]
+
+    def send(r):
+        side = lax.rem(r, DELAY + 1)
+        row_copy(r).wait()
+        for k in range(4):
+            leaving[side, k] = pool[slot_in_pool(plan_s[r, 0, k])]
+            hop(r, k).start()
+
+    def ahead(r):
+        for i in range(SEARCH):
+            balance(st, SEARCH * r + 6 + i)
+        plan_round(st, plan, r + 1, gy)
+        row_copy(r + 1).start()
+
+    def opening(b, carry):
+        brick(b)
+        return carry
+
+    lax.fori_loop(0, 2, opening, 0)
+
+    def early(r, carry):
+        @pl.when(r > DELAY)
+        def _():
+            collect(r - DELAY - 1)
+
+        send(r)
+        ahead(r)
+        brick(r + 2)
+        return carry
+
+    lax.fori_loop(0, 6, early, 0)
+    keep = pltpu.make_async_copy(pool.at[pl.ds(0, OWN)], own_codes, msem.at[2])
+    keep.start()
+
+    def later(r, carry):
+        collect(r - DELAY - 1)
+        send(r)
+        ahead(r)
+        return carry
+
+    lax.fori_loop(6, ROUNDS - 1, later, 0)
+    collect(ROUNDS - DELAY - 2)
+    send(ROUNDS - 1)
+    close_plan(tiles, st, last, flags, gx, gy)
     news = [
         pltpu.make_async_remote_copy(
             flags.at[gx], flags.at[gx], fsend.at[i], frecv.at[i],
@@ -328,83 +492,11 @@
     ]
     for copy in news:
         copy.start()
-    scalars = [
-        pltpu.make_async_copy(plan, plan_s, msem.at[0]),
-        pltpu.make_async_copy(last, last_s, msem.at[1]),
-    ]
-    for copy in scalars:
-        copy.start()
-    for copy in noise:
-        copy.wait()
-    for copy in halos:
-        copy.wait()
-    unpack_halo(F2, yr)
-
-    def brick(b):
-        row, col = b // 4, lax.rem(b, 4)
-
-        def lines(half, carry):
-            for step in range(16):
-                coded = brick_line(F2, NZ, CT, row, col, half, step)
-                for comp in range(2):
-                    place = (PIECES * b + 2 * half + step // 8, pl.ds(32 * (step % 8), 32), pl.ds(128 * comp, 128))
-                    pool[place] = coded[comp]
-            return carry
-
-        lax.fori_loop(0, 2, lines, 0)
-
-    y, z = gy // 4, lax.rem(gy, 4)
-    targets = [
-        4 * y + lax.rem(z + 1, 4),
-        4 * y + lax.rem(z + 3, 4),
-        4 * lax.rem(y + 1, 4) + z,
-        4 * lax.rem(y + 3, 4) + z,
-    ]
-
-    def hop(r, k):
-        side = lax.rem(r, 2)
-        return pltpu.make_async_remote_copy(
-            leaving.at[side, k], landing.at[r, k], ssem.at[side, k], rsem.at[r, k],
-            device_id=(gx, targets[k]), device_id_type=MESH,
-        )
-
-    def collect(r):
-        for k in range(4):
-            copy = hop(r, k)
-            copy.wait()
-            pool[OWN + 4 * r + k] = landing[r, k]
-
-    def send(r):
-        side = lax.rem(r, 2)
-        for k in range(4):
-            leaving[side, k] = pool[slot_in_pool(plan_s[8 * r, k])]
-            hop(r, k).start()
-
-    brick(0)
-    for copy in scalars:
-        copy.wait()
-    send(0)
-    brick(1)
-    send(1)
-
-    def early(r, carry):
-        brick(r)
-        collect(r - 2)
-        send(r)
-        return carry
-
-    lax.fori_loop(2, 8, early, 0)
-    keep = pltpu.make_async_copy(pool.at[pl.ds(0, OWN)], own_codes, msem.at[2])
-    keep.start()
-
-    def later(r, carry):
-        collect(r - 2)
-        send(r)
-        return carry
-
-    lax.fori_loop(8, ROUNDS, later, 0)
-    collect(ROUNDS - 2)
-    collect(ROUNDS - 1)
+    final = pltpu.make_async_copy(last, last_s, msem.at[0])
+    final.start()
+    for r in range(ROUNDS - DELAY - 1, ROUNDS):
+        collect(r)
+    final.wait()
 
     def deliver(s, carry):
         for i in range(PIECES):
@@ -416,13 +508,17 @@
     lax.fori_loop(0, CAPACITY, deliver, 0)
     for copy in news:
         copy.wait()
-    tell = pltpu.make_async_copy(flags, unfinished, msem.at[3])
+    tell = pltpu.make_async_copy(flags, flags_s, msem.at[1])
     tell.start()
     for s in range(CAPACITY):
         part = pl.ds(PIECES * s, PIECES)
         pltpu.make_async_copy(shelf.at[part], mailed.at[part], osem.at[s]).wait()
     keep.wait()
     tell.wait()
+    left = flags_s[0, 0, 0]
+    for g in range(1, 8):
+        left = jnp.maximum(left, flags_s[g, 0, 0])
+    unfinished[0] = left
 
 
 def advance(fields, increments, flow_field, brick_owner):
@@ -434,10 +530,10 @@
         out_shape=(
             jax.ShapeDtypeStruct((CAPACITY * PIECES, *packet), jnp.int16),
             jax.ShapeDtypeStruct((OWN, *packet), jnp.int16),
-            jax.ShapeDtypeStruct((8, 8, 128), jnp.int32),
+            jax.ShapeDtypeStruct((1,), jnp.int32),
         ),
         in_specs=[pl.BlockSpec(memory_space=pltpu.SMEM), any_, any_, any_],
-        out_specs=(any_, any_, any_),
+        out_specs=(any_, any_, pl.BlockSpec(memory_space=pltpu.SMEM)),
         scratch_shapes=[
             pltpu.VMEM((2, 68, PITCH, 128), jnp.float32),
             pltpu.VMEM((NX, NY, 256), jnp.bfloat16),
@@ -449,14 +545,16 @@
             pltpu.VMEM((2, 2, 2, NX, 128), jnp.float32),
             pltpu.VMEM((OWN + 4 * ROUNDS, *packet), jnp.int16),
             pltpu.VMEM((ROUNDS, 4, *packet), jnp.int16),
-            pltpu.VMEM((2, 4, *packet), jnp.int16),
+            pltpu.VMEM((DELAY + 1, 4, *packet), jnp.int16),
             pltpu.VMEM((CAPACITY * PIECES, *packet), jnp.int16),
             pltpu.VMEM((16, 8, 128), jnp.int32),
-            pltpu.VMEM((8 * ROUNDS, 128), jnp.int32),
+            pltpu.VMEM((9, *STATE), jnp.int32),
+            pltpu.VMEM((ROUNDS, 8, 128), jnp.int32),
             pltpu.VMEM((8 * PIECES, 128), jnp.int32),
             pltpu.VMEM((8, 8, 128), jnp.int32),
-            pltpu.SMEM((8 * ROUNDS, 128), jnp.int32),
+            pltpu.SMEM((ROUNDS, 8, 128), jnp.int32),
             pltpu.SMEM((8 * PIECES, 128), jnp.int32),
+            pltpu.SMEM((8, 8, 128), jnp.int32),
             dma((12,)),
             dma((4,)),
             dma((4,)),
@@ -464,8 +562,9 @@
             dma((15,)),
             dma((7,)),
             dma((7,)),
-            dma((4,)),
-            dma((2, 4)),
+            dma((3,)),
+            dma((ROUNDS,)),
+            dma((DELAY + 1, 4)),
             dma((ROUNDS, 4)),
             dma((CAPACITY,)),
         ],
@@ -528,17 +627,32 @@
     return finish(source, arrived, CAPACITY)
 
 
+def spread_kernel(codes, out):
+    out[...] = decode(codes[...]).reshape(out.shape)
+
+
+def spread(mailed):
+    return pl.pallas_call(
+        spread_kernel,
+        out_shape=jax.ShapeDtypeStruct((CAPACITY, EDGE, EDGE, 256), jnp.float32),
+        grid=(CAPACITY,),
+        in_specs=[pl.BlockSpec((PIECES, EDGE * EDGE // PIECES, 256), lambda s: (s, 0, 0))],
+        out_specs=pl.BlockSpec((1, EDGE, EDGE, 256), lambda s: (s, 0, 0, 0)),
+        compiler_params=pltpu.CompilerParams(vmem_limit_bytes=60 * 2**20),
+    )(mailed)
+
+
 def on_device(fields, increments, flow_field, brick_owner):
     mailed, codes, unfinished = advance(fields, increments, flow_field, brick_owner)
 
     def routed():
-        return decode(mailed.reshape(CAPACITY, EDGE, EDGE, 256))
+        return spread(mailed)
 
     def fallback():
         owner_table = lax.all_gather(brick_owner, "gy", axis=1, tiled=True)
         return dense(codes, owner_table, brick_owner)
 
-    return lax.cond(jnp.max(unfinished) == 0, routed, fallback)
+    return lax.cond(unfinished[0] == 0, routed, fallback)
 
 
 def solution(mesh):

time: 113 us -> 92.5 us (0.82)
  other arithmetic: 9.54 us -> 0 us
  Pallas kernels: 98.7 us -> 90.9 us
  local copies, waits for them, and re-layouts: 3.05 us -> 0.01 us
    pallas_call x1, Pallas kernels: 98.7 us -> 83.2 us  [advance(): pl.pallas_call(step_kernel, out_shape=(jax.ShapeDtypeStruct((CAPACITY * P...]
    pallas_call x0 -> x1, Pallas kernels: none -> 7.75 us  [spread(): pl.pallas_call(spread_kernel, out_shape=jax.ShapeDtypeStruct((CAPACITY, E...]
    mul x1 -> x0, other arithmetic: 4.32 us -> none  [decode(): square = square * square * VALUE_MAX]
    unnamed x4 -> x2, local copies, waits for them, and re-layouts: 3.05 us -> 0.01 us
    select_n x1 -> x0, other arithmetic: 1.93 us -> none  [decode(): return jnp.where(part < 0.0, -square, square)]
    lt x1 -> x0, other arithmetic: 1.89 us -> none  [decode(): return jnp.where(part < 0.0, -square, square)]
    reduce_max x1 -> x0, other arithmetic: 1.4 us -> none  [on_device(): return lax.cond(jnp.max(unfinished) == 0, routed, fallback)]
where the time goes in v3:
time: 92.5 us; the launch traced here: 91.6 us
  Pallas kernels  90.9 us (98%)
    pallas_call x1, Pallas kernels, advance(): pl.pallas_call(step_kernel, out_shape=(jax.ShapeDtypeStruct((CAPACITY * P...  83.2 us
    pallas_call x1, Pallas kernels, spread(): pl.pallas_call(spread_kernel, out_shape=jax.ShapeDtypeStruct((CAPACITY, E...  7.75 us

profile of v3, /device:TPU:4, one launch (start us, length us, event | category | flops | bytes accessed | tf_op | source)
XLA Modules:
  0.0 91.6 jit_solution(9210865908466995211)
XLA Ops:
  0.0 0.0 copy-start.1
  0.0 83.2 %shard_map.48 = (s16[28,256,256]{2,1,0:T(8,128)(2,1)}, s16[32,256,256]{2,1,0:T(8,128)(2,1)}, s32[1]{0:T(128)}) custom-call(s32[2,4]{1,0:T(2,128)} %owner.1, f32[64,128,256]{2,1,0:T(8,128)} %fields.1, bf16[64,128,256]{2,1,0:T(8,128)(2,1)} %incr.1, f32[6,64,128]{2,1,0:T(8,128)} %flow.1), custom_call_target="tpu_custom_call" | custom-call | tf_op jit(solution)/shard_map/pallas_call | solution.py:528
  83.8 0.0 copy-done.1
  83.8 7.8 %conditional.1 = (f32[7,32,32,256]{3,2,1,0:T(8,128)}) conditional(s32[]{:T(128)} %bitcast.5, (s32[2,4]{1,0:T(2,128)S(1)}, s16[32,256,256]{2,1,0:T(8,128)(2,1)}) %tuple.17, s16[28,256,256]{2,1,0:T(8,128)(2,1)} %get-tuple-element.20), branch_computations={%region_0.3_spmd, %region_3.4_spmd} | conditional | flops 3744 | bytes 58724500 | solution.py:655
  83.8 7.8 %branch_1_fun.1 = f32[7,32,32,256]{3,2,1,0:T(8,128)} custom-call(s16[28,256,256]{2,1,0:T(8,128)(2,1)} %codes), custom_call_target="tpu_custom_call" | custom-call | tf_op jit(solution)/shard_map/cond/branch_1_fun/pallas_call | solution.py:635
Async XLA Ops:
  0.0 83.8 %copy-start.1 = (s32[2,4]{1,0:T(2,128)S(1)}, s32[2,4]{1,0:T(2,128)}, u32[]{:S(2)}) copy-start(s32[2,4]{1,0:T(2,128)} %owner.1) | copy-start | bytes 100

commit v4 on v3

--- a/solution.py
+++ b/solution.py
@@ -18,9 +18,10 @@
 CAPACITY = 7
 PIECES = 4
 OWN = 8 * PIECES
-ROUNDS = 21
+ROUNDS = 20
 DELAY = 2
 SEARCH = 2
+FIRST_SEARCH = 3
 
 
 def encode(value):
@@ -230,6 +231,22 @@
     return code > 0, number // 8, number % 8
 
 
+def batch_of(brick, piece):
+    low, col = brick // 4, brick % 4
+    inner = jnp.logical_or(col == 1, col == 2)
+    edge = jnp.where(low == 0, jnp.where(piece == 3, 2, 3), jnp.where(piece == 0, 2, 3))
+    middle = jnp.where(piece == 1, 0, jnp.where(piece == 2, 1, edge))
+    return jnp.where(inner, middle, 4 + piece)
+
+
+def packet_of(batch, i):
+    low, m = i // 2, lax.rem(i, 2)
+    brick = jnp.where(batch < 4, 1 + m, 3 * m) + 4 * low
+    edge = jnp.where(batch == 2, 3 - 3 * low, 3 * low)
+    piece = jnp.where(batch < 2, batch + 1, jnp.where(batch < 4, edge, batch - 4))
+    return brick, piece
+
+
 def open_plan(tiles, st):
     src, brick, piece = lanes_of()
     live, dest, _ = decode_tiles(tiles)
@@ -244,7 +261,7 @@
     st[KY_] = jnp.where(ty == 2, tie, jnp.where(ty == 3, 1, 0))
     st[FIRST_] = (piece // 2 + brick) & 1
     st[LOC_] = brick * PIECES + piece
-    st[READY_] = jnp.maximum(brick - 1, 0)
+    st[READY_] = jnp.maximum(batch_of(brick, piece) - 1, 0)
 
 
 def balance(st, t):
@@ -361,9 +378,6 @@
     for peer in col_peers:
         pl.semaphore_signal(barrier, inc=1, device_id=(peer, gy), device_id_type=MESH)
     tiles[gy] = make_tile(owner, gy)
-    for copy in edges:
-        copy.wait()
-    mask_edges(owner, xs, ye, ys)
     pl.semaphore_wait(barrier, 22)
     mail = []
     for i, peer in enumerate(row_peers):
@@ -375,6 +389,9 @@
         )
     for copy in mail:
         copy.start()
+    for copy in edges:
+        copy.wait()
+    mask_edges(owner, xs, ye, ys)
     halos = halo_copies(F, xs, ys, yr, hs, hr)
     for copy in halos:
         copy.start()
@@ -385,39 +402,25 @@
     for copy in block:
         copy.wait()
     mask_block(owner, F2)
-    for copy in mail:
-        copy.wait()
-    open_plan(tiles, st)
-
-    def search(t, carry):
-        balance(st, t)
-        return carry
-
-    lax.fori_loop(0, 6, search, 0)
-
-    def row_copy(r):
-        return pltpu.make_async_copy(plan.at[r], plan_s.at[r], psem.at[r])
-
-    plan_round(st, plan, 0, gy)
-    row_copy(0).start()
     for copy in noise:
         copy.wait()
-    for copy in halos:
-        copy.wait()
-    unpack_halo(F2, yr)
-
-    def brick(b):
-        row, col = b // 4, lax.rem(b, 4)
-
-        def lines(half, carry):
-            for step in range(16):
-                coded = brick_line(F2, NZ, CT, row, col, half, step)
-                for comp in range(2):
-                    place = (PIECES * b + 2 * half + step // 8, pl.ds(32 * (step % 8), 32), pl.ds(128 * comp, 128))
-                    pool[place] = coded[comp]
+
+    def compute(batch):
+        def packet(i, carry):
+            b, piece = packet_of(batch, i)
+            row, col = b // 4, lax.rem(b, 4)
+            for odd in range(2):
+
+                @pl.when(lax.rem(piece, 2) == odd)
+                def _():
+                    for step in range(8):
+                        coded = brick_line(F2, NZ, CT, row, col, piece // 2, 8 * odd + step)
+                        for comp in range(2):
+                            pool[PIECES * b + piece, pl.ds(32 * step, 32), pl.ds(128 * comp, 128)] = coded[comp]
+
             return carry
 
-        lax.fori_loop(0, 2, lines, 0)
+        lax.fori_loop(0, 4, packet, 0)
 
     y, z = gy // 4, lax.rem(gy, 4)
     targets = [
@@ -427,6 +430,9 @@
         4 * lax.rem(y + 3, 4) + z,
     ]
 
+    def row_copy(r):
+        return pltpu.make_async_copy(plan.at[r], plan_s.at[r], psem.at[r])
+
     def hop(r, k):
         side = lax.rem(r, DELAY + 1)
         return pltpu.make_async_remote_copy(
@@ -447,14 +453,28 @@
             leaving[side, k] = pool[slot_in_pool(plan_s[r, 0, k])]
             hop(r, k).start()
 
-    def ahead(r):
-        for i in range(SEARCH):
-            balance(st, SEARCH * r + 6 + i)
+    def ahead(r, steps):
+        for i in range(steps):
+            balance(st, 3 * r + FIRST_SEARCH + i)
         plan_round(st, plan, r + 1, gy)
         row_copy(r + 1).start()
 
-    def opening(b, carry):
-        brick(b)
+    def search(t, carry):
+        balance(st, t)
+        return carry
+
+    def opening(j, carry):
+        compute(j)
+
+        @pl.when(j == 0)
+        def _():
+            for copy in mail:
+                copy.wait()
+            open_plan(tiles, st)
+            lax.fori_loop(0, FIRST_SEARCH, search, 0)
+            plan_round(st, plan, 0, gy)
+            row_copy(0).start()
+
         return carry
 
     lax.fori_loop(0, 2, opening, 0)
@@ -465,8 +485,15 @@
             collect(r - DELAY - 1)
 
         send(r)
-        ahead(r)
-        brick(r + 2)
+        ahead(r, SEARCH)
+        compute(r + 2)
+
+        @pl.when(r == 0)
+        def _():
+            for copy in halos:
+                copy.wait()
+            unpack_halo(F2, yr)
+
         return carry
 
     lax.fori_loop(0, 6, early, 0)
@@ -476,7 +503,7 @@
     def later(r, carry):
         collect(r - DELAY - 1)
         send(r)
-        ahead(r)
+        ahead(r, 3)
         return carry
 
     lax.fori_loop(6, ROUNDS - 1, later, 0)
@@ -627,17 +654,43 @@
     return finish(source, arrived, CAPACITY)
 
 
-def spread_kernel(codes, out):
-    out[...] = decode(codes[...]).reshape(out.shape)
+def spread_kernel(codes, out, taken, made, isem, osem):
+    packets = CAPACITY * PIECES
+
+    def arrive(i):
+        return pltpu.make_async_copy(codes.at[pl.ds(2 * i, 2)], taken.at[pl.ds(2 * i, 2)], isem.at[i])
+
+    def leave(i):
+        return pltpu.make_async_copy(made.at[i], out.at[i // 2, pl.ds(16 * lax.rem(i, 2), 16)], osem.at[i])
+
+    for i in range(packets // 2):
+        arrive(i).start()
+
+    def half(i, carry):
+        arrive(i).wait()
+        for j in range(2):
+            made[i, pl.ds(8 * j, 8)] = decode(taken[2 * i + j]).reshape(8, EDGE, 256)
+        leave(i).start()
+        return carry
+
+    lax.fori_loop(0, packets // 2, half, 0)
+    for i in range(packets // 2):
+        leave(i).wait()
 
 
 def spread(mailed):
+    packets = CAPACITY * PIECES
     return pl.pallas_call(
         spread_kernel,
         out_shape=jax.ShapeDtypeStruct((CAPACITY, EDGE, EDGE, 256), jnp.float32),
-        grid=(CAPACITY,),
-        in_specs=[pl.BlockSpec((PIECES, EDGE * EDGE // PIECES, 256), lambda s: (s, 0, 0))],
-        out_specs=pl.BlockSpec((1, EDGE, EDGE, 256), lambda s: (s, 0, 0, 0)),
+        in_specs=[pl.BlockSpec(memory_space=pl.ANY)],
+        out_specs=pl.BlockSpec(memory_space=pl.ANY),
+        scratch_shapes=[
+            pltpu.VMEM((packets, EDGE * EDGE // PIECES, 256), jnp.int16),
+            pltpu.VMEM((packets // 2, 16, EDGE, 256), jnp.float32),
+            pltpu.SemaphoreType.DMA((packets // 2,)),
+            pltpu.SemaphoreType.DMA((packets // 2,)),
+        ],
         compiler_params=pltpu.CompilerParams(vmem_limit_bytes=60 * 2**20),
     )(mailed)
 

time: 92.5 us -> 84.3 us (0.911)
  Pallas kernels: 90.9 us -> 83.3 us
    pallas_call x1, Pallas kernels: 83.2 us -> 78.9 us  [advance(): pl.pallas_call(step_kernel, out_shape=(jax.ShapeDtypeStruct((CAPACITY * P...]
    pallas_call x1, Pallas kernels: 7.75 us -> 4.45 us  [spread(): pl.pallas_call(spread_kernel, out_shape=jax.ShapeDtypeStruct((CAPACITY, E...]
where the time goes in v4:
time: 84.3 us; the launch traced here: 84 us
  Pallas kernels  83.3 us (99%)
    pallas_call x1, Pallas kernels, advance(): pl.pallas_call(step_kernel, out_shape=(jax.ShapeDtypeStruct((CAPACITY * P...  78.9 us
    pallas_call x1, Pallas kernels, spread(): pl.pallas_call(spread_kernel, out_shape=jax.ShapeDtypeStruct((CAPACITY, E...  4.45 us

profile of v4, /device:TPU:4, one launch (start us, length us, event | category | flops | bytes accessed | tf_op | source)
XLA Modules:
  0.0 84.0 jit_solution(3325558198356331503)
XLA Ops:
  0.0 0.0 copy-start.1
  0.0 78.9 %shard_map.48 = (s16[28,256,256]{2,1,0:T(8,128)(2,1)}, s16[32,256,256]{2,1,0:T(8,128)(2,1)}, s32[1]{0:T(128)}) custom-call(s32[2,4]{1,0:T(2,128)} %owner.1, f32[64,128,256]{2,1,0:T(8,128)} %fields.1, bf16[64,128,256]{2,1,0:T(8,128)(2,1)} %incr.1, f32[6,64,128]{2,1,0:T(8,128)} %flow.1), custom_call_target="tpu_custom_call" | custom-call | tf_op jit(solution)/shard_map/pallas_call | solution.py:555
  79.5 0.0 copy-done.1
  79.5 4.5 %conditional.1 = (f32[7,32,32,256]{3,2,1,0:T(8,128)}) conditional(s32[]{:T(128)} %bitcast.5, (s32[2,4]{1,0:T(2,128)S(1)}, s16[32,256,256]{2,1,0:T(8,128)(2,1)}) %tuple.17, s16[28,256,256]{2,1,0:T(8,128)(2,1)} %get-tuple-element.20), branch_computations={%region_0.3_spmd, %region_3.4_spmd} | conditional | flops 3744 | bytes 58724500 | solution.py:708
  79.6 4.4 %branch_1_fun.1 = f32[7,32,32,256]{3,2,1,0:T(8,128)} custom-call(s16[28,256,256]{2,1,0:T(8,128)(2,1)} %codes), custom_call_target="tpu_custom_call" | custom-call | tf_op jit(solution)/shard_map/cond/branch_1_fun/pallas_call | solution.py:683
Async XLA Ops:
  0.0 79.5 %copy-start.1 = (s32[2,4]{1,0:T(2,128)S(1)}, s32[2,4]{1,0:T(2,128)}, u32[]{:S(2)}) copy-start(s32[2,4]{1,0:T(2,128)} %owner.1) | copy-start | bytes 100

commit v5 on v4

--- a/solution.py
+++ b/solution.py
@@ -20,7 +20,7 @@
 OWN = 8 * PIECES
 ROUNDS = 20
 DELAY = 2
-SEARCH = 2
+SEARCH = 1
 FIRST_SEARCH = 3
 
 

time: 84.3 us -> 83.1 us (0.986)
  Pallas kernels: 83.3 us -> 82.2 us
    pallas_call x1, Pallas kernels: 78.9 us -> 77.8 us  [advance(): pl.pallas_call(step_kernel, out_shape=(jax.ShapeDtypeStruct((CAPACITY * P...]
where the time goes in v5:
time: 83.1 us; the launch traced here: 82.9 us
  Pallas kernels  82.2 us (99%)
    pallas_call x1, Pallas kernels, advance(): pl.pallas_call(step_kernel, out_shape=(jax.ShapeDtypeStruct((CAPACITY * P...  77.8 us
    pallas_call x1, Pallas kernels, spread(): pl.pallas_call(spread_kernel, out_shape=jax.ShapeDtypeStruct((CAPACITY, E...  4.45 us

profile of v5, /device:TPU:4, one launch (start us, length us, event | category | flops | bytes accessed | tf_op | source)
XLA Modules:
  0.0 82.9 jit_solution(9676646789098452301)
XLA Ops:
  0.0 0.0 copy-start.1
  0.0 77.8 %shard_map.48 = (s16[28,256,256]{2,1,0:T(8,128)(2,1)}, s16[32,256,256]{2,1,0:T(8,128)(2,1)}, s32[1]{0:T(128)}) custom-call(s32[2,4]{1,0:T(2,128)} %owner.1, f32[64,128,256]{2,1,0:T(8,128)} %fields.1, bf16[64,128,256]{2,1,0:T(8,128)(2,1)} %incr.1, f32[6,64,128]{2,1,0:T(8,128)} %flow.1), custom_call_target="tpu_custom_call" | custom-call | tf_op jit(solution)/shard_map/pallas_call | solution.py:555
  78.4 0.0 copy-done.1
  78.5 4.5 %conditional.1 = (f32[7,32,32,256]{3,2,1,0:T(8,128)}) conditional(s32[]{:T(128)} %bitcast.5, (s32[2,4]{1,0:T(2,128)S(1)}, s16[32,256,256]{2,1,0:T(8,128)(2,1)}) %tuple.17, s16[28,256,256]{2,1,0:T(8,128)(2,1)} %get-tuple-element.20), branch_computations={%region_0.3_spmd, %region_3.4_spmd} | conditional | flops 3744 | bytes 58724500 | solution.py:708
  78.5 4.4 %branch_1_fun.1 = f32[7,32,32,256]{3,2,1,0:T(8,128)} custom-call(s16[28,256,256]{2,1,0:T(8,128)(2,1)} %codes), custom_call_target="tpu_custom_call" | custom-call | tf_op jit(solution)/shard_map/cond/branch_1_fun/pallas_call | solution.py:683
Async XLA Ops:
  0.0 78.4 %copy-start.1 = (s32[2,4]{1,0:T(2,128)S(1)}, s32[2,4]{1,0:T(2,128)}, u32[]{:S(2)}) copy-start(s32[2,4]{1,0:T(2,128)} %owner.1) | copy-start | bytes 100
